TPU v7x, 256 devices: a whole 4x4x8 slice. The times are simulated.
256 devices in a mesh: kv: 64 (over y, z_lo, x), req: 4 (over z_hi, core).
Axes of the slice: x: 4, y: 4, z: 8 (z_hi: 2, z_lo: 4; z = z_hi * 4 + z_lo), core: 2. Of those that a mesh axis runs over, the one named last changes fastest.
Arguments:
- q_nope: bfloat16 [2, 4, 128, 128], P(None, 'req', 'kv'), parts along dimension 1, may hold values from -6 to 6
- q_rope: bfloat16 [2, 4, 128, 64], P(None, 'req', 'kv'), parts along dimension 1, may hold values from -12 to 12
- uk_weight: bfloat16 [128, 128, 512], P('kv'), may hold values from -0.5 to 0.5
- uv_weight: bfloat16 [128, 512, 128], P('kv'), may hold values from -0.25 to 0.25
- out_weight: bfloat16 [16384, 7168], P('kv'), may hold values from -0.125 to 0.125
- cache: bfloat16 [4, 131072, 576], P('req', 'kv'), parts along dimension 0, may hold values from -12 to 12
- new_rows: bfloat16 [2, 4, 576], P(None, 'req'), parts along dimension 1, may hold values from -12 to 12
- context_len: int32 [4], P('req'), parts along dimension 0, may hold values from 32768 to 131070, as said below
Outputs:
- attended: bfloat16 [2, 4, 7168], P(None, 'req', 'kv'), parts along dimension 1
There are 4 independent parts, one for each index of `req`. A program takes and returns all parts, laid end to end along the dimension named above; an argument that names none is the same for every part. Nothing has to cross between parts.
Inputs may be any that keep to these rules, and one draw needn't show every extreme that they name: `context_len`: each request has at least 32768 cached tokens; in every draw, over all request groups, the longest request has exactly 131070.
All inputs are finite; a program needn't handle non-finite values.
Results may differ from a plain program's by a relative error of at most 0.02.
Values may be sent and summed in bfloat16 or wider, within the bound.
A program may use at most 128 MiB of HBM per device.

v0:
```python
import jax
import jax.numpy as jnp
from jax import lax
from jax.sharding import PartitionSpec as P


def merged(value, axis, combine):
    everything = jax.tree.map(lambda part: lax.all_gather(part, axis), value)
    leading = jax.tree.map(lambda part: part[0], everything)

    def turn(k, so_far):
        return combine(so_far, jax.tree.map(lambda part: part[k], everything))

    return lax.fori_loop(1, lax.axis_size(axis), turn, leading)


def absorb(nope_part, rope_part, uk_weight):
    latent = jnp.einsum(
        "...hn,hnl->...hl", nope_part, uk_weight, preferred_element_type=jnp.float32
    )
    return jnp.concatenate([latent.astype(jnp.bfloat16), rope_part], axis=-1)


def project(head_latent, uv_weight, out_weight):
    head_value = jnp.einsum(
        "bhl,hlv->bhv", head_latent, uv_weight, preferred_element_type=jnp.float32
    ).astype(jnp.bfloat16)
    flat = head_value.reshape(head_value.shape[0], head_value.shape[1] * head_value.shape[2])
    return jnp.dot(flat, out_weight, preferred_element_type=jnp.float32)


def softmax_join(first, second):
    out_a, peak_a, total_a = first
    out_b, peak_b, total_b = second
    peak = jnp.maximum(peak_a, peak_b)
    factor_a = jnp.exp(peak_a - peak)
    factor_b = jnp.exp(peak_b - peak)
    joined = out_a * factor_a[..., None] + out_b * factor_b[..., None]
    return (joined, peak, total_a * factor_a + total_b * factor_b)


def body(q_nope, q_rope, uk_weight, uv_weight, out_weight, cache, new_rows, context_len):
    kv_count = lax.axis_size("kv")
    own_index = lax.axis_index("kv")
    local_rows = cache.shape[1]
    latent_width = uv_weight.shape[1]
    head_count = uk_weight.shape[0]
    scale = (q_nope.shape[3] + q_rope.shape[3]) ** (-0.5)
    tokens = jnp.arange(local_rows, dtype=jnp.int32) * kv_count + own_index
    cache_valid = tokens[None, :] < context_len[:, None]
    latents = cache[:, :, :latent_width]
    results = []
    for step in range(q_nope.shape[0]):
        queries = lax.all_gather(
            absorb(q_nope[step], q_rope[step], uk_weight), "kv", axis=1, tiled=True
        )
        appended = new_rows[: step + 1]
        offsets = jnp.arange(step + 1, dtype=jnp.int32)
        owner = (context_len[None, :] + offsets[:, None]) % kv_count == own_index
        cache_scores = (
            jnp.einsum("bhw,bcw->bhc", queries, cache, preferred_element_type=jnp.float32) * scale
        )
        new_scores = (
            jnp.einsum("bhw,kbw->bhk", queries, appended, preferred_element_type=jnp.float32)
            * scale
        )
        cache_scores = jnp.where(cache_valid[:, None, :], cache_scores, -1e30)
        new_scores = jnp.where(owner.T[:, None, :], new_scores, -1e30)
        peak = jnp.maximum(jnp.max(cache_scores, axis=-1), jnp.max(new_scores, axis=-1))
        cache_expo = jnp.exp(cache_scores - peak[..., None])
        new_expo = jnp.exp(new_scores - peak[..., None])
        total = jnp.sum(cache_expo, axis=-1) + jnp.sum(new_expo, axis=-1)
        partial_value = jnp.einsum(
            "bhc,bcl->bhl",
            cache_expo.astype(jnp.bfloat16),
            latents,
            preferred_element_type=jnp.float32,
        )
        partial_value = partial_value + jnp.einsum(
            "bhk,kbl->bhl",
            new_expo.astype(jnp.bfloat16),
            appended[:, :, :latent_width],
            preferred_element_type=jnp.float32,
        )
        joined, joined_peak, joined_total = merged((partial_value, peak, total), "kv", softmax_join)
        whole = (joined / joined_total[..., None]).astype(jnp.bfloat16)
        owned = lax.dynamic_slice_in_dim(whole, own_index * head_count, head_count, 1)
        term = project(owned, uv_weight, out_weight)
        results.append(
            lax.psum_scatter(term, "kv", scatter_dimension=1, tiled=True).astype(jnp.bfloat16)
        )
    return jnp.stack(results, axis=0)


def solution(mesh):
    in_specs = (
        P(None, "req", "kv", None),
        P(None, "req", "kv", None),
        P("kv", None, None),
        P("kv", None, None),
        P("kv", None),
        P("req", "kv", None),
        P(None, "req", None),
        P("req"),
    )
    out_specs = P(None, "req", "kv")
    return jax.shard_map(body, mesh=mesh, in_specs=in_specs, out_specs=out_specs, check_vma=False)
```

profile of v0, /device:TPU:2, one launch (start us, length us, event | category | flops | bytes accessed | tf_op | source)
XLA Modules:
  0.0 2012.2 jit_solution(16869732476067823405)
XLA Ops:
  8.9 182.9 %all_gather.39 = bf16[1,128,576]{2,0,1:T(2,128)(2,1)S(1)} all-gather(bf16[1,2,576]{2,0,1:T(2,128)(2,1)S(1)} %copy.20), channel_id=1, replica_groups=mesh['kv'=64,'req'=4] {'kv'}, dimensions={1}, use_global_device_ids=true | all-gather | bytes 149760 | tf_op jit(solution)/shard_map/all_gather | solution.py:54
  192.9 2.4 fusion.75
  196.2 1.6 fusion.29
  198.1 187.9 %all_gather.34 = bf16[1,128,576]{2,0,1:T(2,128)(2,1)S(1)} all-gather(bf16[1,2,576]{2,0,1:T(2,128)(2,1)S(1)} %copy.17), channel_id=1, replica_groups=mesh['kv'=64,'req'=4] {'kv'}, dimensions={1}, use_global_device_ids=true | all-gather | bytes 149760 | tf_op jit(solution)/shard_map/all_gather | solution.py:54
  387.9 1.6 fusion.26
  389.5 1.5 fusion.37
  391.1 1.5 fusion.35
  392.6 177.7 %all-gather.9 = f32[64,1,128]{2,1,0:T(1,128)S(1)} all-gather(f32[1,1,128]{2,1,0:T(1,128)S(1)} %add_bitcast_fusion), channel_id=7, replica_groups=mesh['kv'=64,'req'=4] {'kv'}, dimensions={0}, use_global_device_ids=true | all-gather | bytes 33280 | tf_op jit(solution)/shard_map/all_gather | solution.py:8
  570.3 180.1 %all-gather.8 = f32[64,1,128]{2,1,0:T(1,128)S(1)} all-gather(f32[1,1,128]{2,1,0:T(1,128)S(1)} %bitcast.221), channel_id=6, replica_groups=mesh['kv'=64,'req'=4] {'kv'}, dimensions={0}, use_global_device_ids=true | all-gather | bytes 33280 | tf_op jit(solution)/shard_map/all_gather | solution.py:8
  750.4 177.9 %all-gather.7 = f32[64,1,128]{2,1,0:T(1,128)S(1)} all-gather(f32[1,1,128]{2,1,0:T(1,128)S(1)} %add_bitcast_fusion.1), channel_id=4, replica_groups=mesh['kv'=64,'req'=4] {'kv'}, dimensions={0}, use_global_device_ids=true | all-gather | bytes 33280 | tf_op jit(solution)/shard_map/all_gather | solution.py:8
  928.2 179.8 %all-gather.6 = f32[64,1,128]{2,1,0:T(1,128)S(1)} all-gather(f32[1,1,128]{2,1,0:T(1,128)S(1)} %bitcast.222), channel_id=3, replica_groups=mesh['kv'=64,'req'=4] {'kv'}, dimensions={0}, use_global_device_ids=true | all-gather | bytes 33280 | tf_op jit(solution)/shard_map/all_gather | solution.py:8
  1109.0 72.7 %while.39 = (s32[]{:T(128)}, f32[1,128,512]{2,1,0:T(8,128)S(1)}, f32[1,128]{1,0:T(1,128)S(1)}, f32[1,128]{1,0:T(1,128)S(1)}, f32[64,1,128]{2,1,0:T(1,128)S(1)}, ...) while((s32[]{:T(128)}, f32[1,128,512]{2,1,0:T(8,128)S(1)}, ...), condition=%wide.region_10.11_spmd, body=%wide.region_9.10_spmd.sunk | while | flops 197637 | bytes 794259 | solution.py:14
  1182.8 72.8 %while.38 = (s32[]{:T(128)}, f32[1,128,512]{2,1,0:T(8,128)S(1)}, f32[1,128]{1,0:T(1,128)S(1)}, f32[1,128]{1,0:T(1,128)S(1)}, f32[64,1,128]{2,1,0:T(1,128)S(1)}, ...) while((s32[]{:T(128)}, f32[1,128,512]{2,1,0:T(8,128)S(1)}, ...), condition=%wide.region_3.4_spmd, body=%wide.region_2.3_spmd.sunk | while | flops 197637 | bytes 794259 | solution.py:14
  1187.5 1.1 fusion.94
  1194.4 1.1 fusion.94
  1195.5 1.1 fusion.94
  1201.3 1.1 fusion.94
  1202.5 1.1 fusion.94
  1209.4 1.1 fusion.94
  1216.3 1.1 fusion.94
  1217.5 1.1 fusion.94
  1223.3 1.1 fusion.94
  1224.4 1.1 fusion.94
  1231.4 1.1 fusion.94
  1238.3 1.1 fusion.94
  1239.4 1.1 fusion.94
  1245.2 1.1 fusion.94
  1246.4 1.1 fusion.94
  1256.1 5.4 convolution_bitcast_fusion.1
  1261.6 5.4 convolution_bitcast_fusion
  1267.0 362.0 %reduce-scatter.7.cloned.1.call-done = f32[112,1]{1,0:T(8,128)} async-done(((f32[7168,1]{1,0:T(8,128)}), f32[112,1]{1,0:T(8,128)}) %reduce-scatter.7.cloned.1.call-update) | async-done | bytes 464
  1629.9 374.3 %reduce-scatter.9.cloned.1.call-done = f32[112,1]{1,0:T(8,128)} async-done(((f32[7168,1]{1,0:T(8,128)}), f32[112,1]{1,0:T(8,128)}) %reduce-scatter.9.cloned.1.call-update) | async-done | bytes 464
  (555 shorter events, 134.8 us)
Async XLA Ops:
  6.5 2.2 copy-start
  6.5 188.7 %copy-start.5 = (bf16[2,1,576]{2,0,1:T(2,128)(2,1)S(1)}, bf16[2,1,576]{2,0,1:T(2,128)(2,1)}, u32[]{:S(2)}) copy-start(bf16[2,1,576]{2,0,1:T(2,128)(2,1)} %param.18) | copy-start | bytes 6916
  6.5 189.7 %copy-start.1 = (bf16[1,2048,576]{1,2,0:T(8,128)(2,1)S(1)}, bf16[1,2048,576]{1,2,0:T(8,128)(2,1)}, u32[]{:S(2)}) copy-start(bf16[1,2048,576]{1,2,0:T(8,128)(2,1)} %param.17) | copy-start | bytes 7077892
  6.5 1101.5 %all-gather.15.cloned.1.call-start = ((), (), s32[]{:S(2)}) async-start(), calls=%async_computation.3 | async-start | bytes 17039360 | tf_op jit(solution)/shard_map/all_gather | solution.py:8
  195.2 1.0 copy-start.2
  197.8 984.0 %all-gather.13.cloned.1.call-start = ((), (), s32[]{:S(2)}) async-start(), calls=%async_computation.2 | async-start | bytes 17039360 | tf_op jit(solution)/shard_map/all_gather | solution.py:8
  386.8 1.0 copy-start.3
  389.5 1239.6 %reduce-scatter.7.cloned.1.call-start = ((), (), s32[]{:S(2)}) async-start(), calls=%async_computation.4 | async-start | bytes 3727360
  1109.0 146.8 %copy-start.4 = (bf16[2,512,128]{2,1,0:T(8,128)(2,1)S(1)}, bf16[2,512,128]{2,1,0:T(8,128)(2,1)}, u32[]{:S(2)}) copy-start(bf16[2,512,128]{2,1,0:T(8,128)(2,1)} %param.15) | copy-start | bytes 786436
  1261.6 742.6 %reduce-scatter.9.cloned.1.call-start = ((), (), s32[]{:S(2)}) async-start(), calls=%async_computation.5 | async-start | bytes 3727360
Sparse Core Ops, SparseCore 0:
  197.9 380.7 all-gather.14
  580.5 378.0 all-gather.12
  1261.7 367.3 reduce-scatter.6
  1631.6 372.6 reduce-scatter.8
where the time goes:
time: 2020 us; the launch traced here: 2010 us
  blocking collectives  1090 us (54%)
  waiting for transfers between devices  736 us (36%)
  other arithmetic  145 us (7%)
    unnamed x6, waiting for transfers between devices  736 us
    all_gather x4, blocking collectives, merged(): everything = jax.tree.map(lambda part: lax.all_gather(part, axis), value)  715 us
    all_gather x2, blocking collectives, body(): lax.all_gather(absorb(q_nope[step], q_rope[step], uk_weight), 'kv', axis=...  371 us
    add x126, other arithmetic, softmax_join(): joined = out_a * factor_a[..., None] + out_b * factor_b[..., None]  135 us
  transfers between devices with their start and end apart: 4, of which 2 were waited for; matrix products, arithmetic and copies ran while one was open for 4% of the time, Pallas kernels for 0%

commit v1 on v0

v1 whole, which is shorter than its diff:
```python
import functools
import math

import jax
import jax.numpy as jnp
from jax import lax
from jax.experimental import pallas as pl
from jax.experimental.pallas import tpu as pltpu
from jax.sharding import PartitionSpec as P

MESH = pl.DeviceIdType.MESH
F32 = jnp.float32
BF16 = jnp.bfloat16

SIDE = 4
HOLD = 2
STEPS = 2
ROWS = HOLD * STEPS
LAT = 512
ROPE = 64
WIDE = LAT + ROPE
WIDE_PAD = 640
NEVER = -1e30

RING = [(dy, dx) for dy in range(SIDE) for dx in range(SIDE) if dy or dx]
RING.sort(key=lambda d: -(min(d[0], SIDE - d[0]) + min(d[1], SIDE - d[1])))
LINE = (3, 2, 1)


def split(value):
    high = value.astype(BF16).astype(F32)
    return high, (value - high).astype(BF16).astype(F32)


def with_stats(peak, total, rows):
    lane = lax.broadcasted_iota(jnp.int32, (rows, 128), 1)
    result = jnp.zeros((rows, 128), F32)
    for at, part in enumerate((*split(peak), *split(total))):
        result = jnp.where(lane == at, part, result)
    return result


def join(parts, pick, out_rows):
    stats = parts[:, LAT:].astype(F32).T
    peak = stats[0:1] + stats[1:2]
    total = stats[2:3] + stats[3:4]
    n = parts.shape[0]
    peaks = jnp.where(pick, jnp.broadcast_to(peak, (out_rows, n)), -3e38)
    top = jnp.max(peaks, axis=1, keepdims=True)
    factor = jnp.where(pick, jnp.exp2(peaks - top), 0.0)
    whole = jnp.sum(factor * total, axis=1, keepdims=True)
    high, low = split(factor)
    both = jnp.concatenate([high, low], axis=0).astype(BF16)
    summed = jnp.dot(both, parts[:, :LAT], preferred_element_type=F32)
    return summed[:out_rows] + summed[out_rows:], top, whole


def kernel(
    q_nope, q_rope, uk, uv, out_w, cache, new_rows, context, out,
    qn_v, qr_v, uk_v, uv_v, w_v, c_v, new_v, ctx_s, qx, zq, q_all, keys, scores, ob, rb, rb2, ts, tr,
    load_sem, send_sem, recv_sem,
):
    me = lax.axis_index("kv")
    y, z, x = me // 16, (me // 4) % 4, me % 4
    plane = y * 4 + x
    in_plane = [((y + dy) % 4, (x + dx) % 4) for dy, dx in RING]
    in_line = [(z + dz) % 4 for dz in LINE]

    def plane_id(peer):
        return {"kv": peer[0] * 16 + z * 4 + peer[1]}

    def line_id(peer):
        return {"kv": y * 16 + peer * 4 + x}

    barrier = pltpu.get_barrier_semaphore()
    for peer in in_plane:
        pl.semaphore_signal(barrier, inc=1, device_id=plane_id(peer), device_id_type=MESH)
    for peer in in_line:
        pl.semaphore_signal(barrier, inc=1, device_id=line_id(peer), device_id_type=MESH)

    loads = [
        pltpu.make_async_copy(src, dst, load_sem.at[k])
        for k, (src, dst) in enumerate(
            [(q_nope, qn_v), (q_rope, qr_v), (uk, uk_v), (context, ctx_s), (new_rows, new_v), (cache.at[0], c_v), (uv, uv_v), (out_w, w_v)]
        )
    ]
    for load in loads:
        load.start()
    l_qn, l_qr, l_uk, l_ctx, l_new, l_cache, l_uv, l_w = loads

    l_qn.wait()
    l_qr.wait()
    l_uk.wait()
    qx[...] = jnp.zeros((8, 128), F32)
    for step in range(STEPS):
        qx[step * 2 : step * 2 + 2, :] = qn_v[step, 0].astype(F32)
    lhs = qx[...].astype(BF16)
    even = lax.broadcasted_iota(jnp.int32, (8, 1), 0) % 2 == 0
    lat = jnp.where(
        even,
        jnp.dot(lhs, uk_v[0], preferred_element_type=F32),
        jnp.dot(lhs, uk_v[1], preferred_element_type=F32),
    )
    zq[z, 0:4, 0:LAT] = lat[0:4].astype(BF16).astype(F32)
    lane = lax.broadcasted_iota(jnp.int32, (2, ROPE), 1)
    for step in range(STEPS):
        flag = jnp.where(lane == step, 1.0, 0.0).astype(F32)
        zq[z, step * 2 : step * 2 + 2, LAT:] = jnp.concatenate(
            [qr_v[step, 0].astype(F32), flag], axis=1
        )

    pl.semaphore_wait(barrier, len(in_plane) + len(in_line))

    def remote(src, dst, phase, device):
        copy = pltpu.make_async_remote_copy(
            src_ref=src,
            dst_ref=dst,
            send_sem=send_sem.at[phase],
            recv_sem=recv_sem.at[phase],
            device_id=device,
            device_id_type=MESH,
        )
        copy.start()

    def take(ref, sem):
        pltpu.make_async_copy(ref, ref, sem).wait()

    mine = zq.at[z, pl.ds(0, 4)]
    for peer in in_line:
        remote(mine, mine, 0, line_id(peer))

    l_ctx.wait()
    l_new.wait()
    l_cache.wait()
    length = ctx_s[0]

    def prepare(k, _):
        base = pl.multiple_of(k * 256, 256)
        token = (lax.broadcasted_iota(jnp.int32, (256, 1), 0) + base) * 64 + me
        block = c_v[pl.ds(base, 256), :].astype(F32)
        for step in range(STEPS):
            block = jnp.where(token == length + step, new_v[step].astype(F32), block)
        lane = lax.broadcasted_iota(jnp.int32, (256, WIDE_PAD - WIDE), 1)
        mask = jnp.where((lane < STEPS) & (token > length + lane), NEVER, 0.0)
        keys[pl.ds(base, 256), :] = jnp.concatenate([block, mask], axis=1).astype(BF16)
        return 0

    lax.fori_loop(0, 4, prepare, 0)

    take(zq.at[pl.ds(0, 3), pl.ds(0, 4)], recv_sem.at[0])
    mine = q_all.at[pl.ds(pl.multiple_of(plane * 16, 16), 16)]
    mine[...] = jnp.concatenate([zq[k, 0:4, :] for k in range(4)], axis=0).astype(BF16)
    for peer in in_plane:
        remote(mine, mine, 1, plane_id(peer))
    lax.fori_loop(4, 8, prepare, 0)
    take(q_all.at[pl.ds(0, 240)], recv_sem.at[1])

    scale = math.log2(math.e) * (128 + ROPE) ** -0.5
    queries = q_all[...]
    peak = None
    for k in range(4):
        part = lax.dot_general(
            queries, keys[k * 512 : k * 512 + 512, :], (((1,), (1,)), ((), ())), preferred_element_type=F32
        )
        scores[:, k * 512 : k * 512 + 512] = part
        for j in range(4):
            tile = part[:, j * 128 : j * 128 + 128]
            peak = tile if peak is None else jnp.maximum(peak, tile)
    high, low = split(jnp.max(peak, axis=1, keepdims=True) * scale)
    peak = high + low
    total = jnp.zeros((256, 128), F32)
    value = jnp.zeros((256, LAT), F32)
    for k in range(4):
        expo = jnp.exp2(scores[:, k * 512 : k * 512 + 512] * scale - peak)
        for j in range(4):
            total = total + expo[:, j * 128 : j * 128 + 128]
        value = value + jnp.dot(
            expo.astype(BF16), keys[k * 512 : k * 512 + 512, 0:LAT], preferred_element_type=F32
        )
    ob[:, 0:LAT] = value.astype(BF16)
    ob[:, LAT:] = with_stats(peak, jnp.sum(total, axis=1, keepdims=True), 256).astype(BF16)

    mine = pl.ds(pl.multiple_of(plane * 16, 16), 16)
    for peer in in_plane:
        theirs = pl.ds(pl.multiple_of((peer[0] * 4 + peer[1]) * 16, 16), 16)
        remote(ob.at[theirs], rb.at[mine], 2, plane_id(peer))
    rb[mine, :] = ob[mine, :]
    take(rb.at[pl.ds(0, 240)], recv_sem.at[2])
    pick = (
        lax.broadcasted_iota(jnp.int32, (16, 256), 1) % 16
        == lax.broadcasted_iota(jnp.int32, (16, 256), 0)
    )
    summed, top, whole = join(rb[...], pick, 16)
    mine = rb2.at[pl.ds(pl.multiple_of(z * 16, 16), 16)]
    mine[...] = jnp.concatenate([summed, with_stats(top, whole, 16)], axis=1).astype(BF16)
    for peer in in_line:
        remote(mine, mine, 3, line_id(peer))
    l_uv.wait()
    l_w.wait()
    take(rb2.at[pl.ds(0, 48)], recv_sem.at[3])
    pick = lax.broadcasted_iota(jnp.int32, (8, 64), 1) % 16 == z * 4 + (
        lax.broadcasted_iota(jnp.int32, (8, 64), 0) % 4
    )
    summed, top, whole = join(rb2[...], pick, 8)
    latent = (summed / whole).astype(BF16)

    head_value = jnp.concatenate(
        [
            jnp.where(even, jnp.dot(latent, uv_v[0], preferred_element_type=F32), 0.0),
            jnp.where(even, 0.0, jnp.dot(latent, uv_v[1], preferred_element_type=F32)),
        ],
        axis=1,
    )
    pairs = head_value + pltpu.roll(head_value, 7, 0)
    first = lax.broadcasted_iota(jnp.int32, (8, 1), 0) == 0
    flat = jnp.where(first, pairs, pltpu.roll(pairs, 7, 0)).astype(BF16)
    for i in (4, 3, 5, 2, 6, 1, 7, 0):
        group = (me // 8 + i) % 8
        columns = pl.ds(pl.multiple_of(group * 896, 128), 896)
        term = jnp.dot(flat, w_v[:, columns], preferred_element_type=F32)
        for j in range(8):
            ts[group * 8 + j, :, 0:112] = term[:, j * 112 : j * 112 + 112]
        for j in range(8):
            peer = group * 8 + (me + j) % 8
            if i == 0 and j == 0:
                tr[me, 0:2, :] = ts[me, 0:2, :]
            else:
                remote(ts.at[peer, pl.ds(0, 2)], tr.at[me, pl.ds(0, 2)], 4, {"kv": peer})
    take(tr.at[pl.ds(0, 63), pl.ds(0, 2)], recv_sem.at[4])
    result = jnp.sum(tr[:, 0:2, :], axis=0)
    out[:, 0, :] = result[:, 0:112].astype(BF16)

    take(zq.at[pl.ds(0, 3), pl.ds(0, 4)], send_sem.at[0])
    take(q_all.at[pl.ds(0, 240)], send_sem.at[1])
    take(ob.at[pl.ds(0, 240)], send_sem.at[2])
    take(rb2.at[pl.ds(0, 48)], send_sem.at[3])
    take(ts.at[pl.ds(0, 63), pl.ds(0, 2)], send_sem.at[4])


def body(*args):
    any_space = pl.BlockSpec(memory_space=pl.ANY)
    return pl.pallas_call(
        kernel,
        out_shape=jax.ShapeDtypeStruct((STEPS, 1, 112), BF16),
        in_specs=[any_space] * 8,
        out_specs=pl.BlockSpec(memory_space=pltpu.VMEM),
        scratch_shapes=[
            pltpu.VMEM((2, 1, 2, 128), BF16),
            pltpu.VMEM((2, 1, 2, ROPE), BF16),
            pltpu.VMEM((2, 128, LAT), BF16),
            pltpu.VMEM((2, LAT, 128), BF16),
            pltpu.VMEM((256, 7168), BF16),
            pltpu.VMEM((2048, WIDE), BF16),
            pltpu.VMEM((2, 1, WIDE), BF16),
            pltpu.SMEM((1,), jnp.int32),
            pltpu.VMEM((8, 128), F32),
            pltpu.VMEM((4, 8, WIDE_PAD), F32),
            pltpu.VMEM((256, WIDE_PAD), BF16),
            pltpu.VMEM((2048, WIDE_PAD), BF16),
            pltpu.VMEM((256, 2048), F32),
            pltpu.VMEM((256, WIDE_PAD), BF16),
            pltpu.VMEM((256, WIDE_PAD), BF16),
            pltpu.VMEM((64, WIDE_PAD), BF16),
            pltpu.VMEM((64, 8, 128), F32),
            pltpu.VMEM((64, 8, 128), F32),
            pltpu.SemaphoreType.DMA((8,)),
            pltpu.SemaphoreType.DMA((5,)),
            pltpu.SemaphoreType.DMA((5,)),
        ],
        compiler_params=pltpu.CompilerParams(
            collective_id=0, has_side_effects=True, vmem_limit_bytes=48 << 20
        ),
    )(*args)


def solution(mesh):
    in_specs = (
        P(None, "req", "kv", None),
        P(None, "req", "kv", None),
        P("kv", None, None),
        P("kv", None, None),
        P("kv", None),
        P("req", "kv", None),
        P(None, "req", None),
        P("req"),
    )
    return jax.shard_map(body, mesh=mesh, in_specs=in_specs, out_specs=P(None, "req", "kv"), check_vma=False)
```

time: 2020 us -> 41.3 us (0.02)
  blocking collectives: 1090 us -> 0 us
  waiting for transfers between devices: 736 us -> 0 us
  other arithmetic: 145 us -> 0 us
  Pallas kernels: 0 us -> 35.9 us
    all_gather x6 -> x0, blocking collectives: 1090 us -> none  [the longest x4 715 us: merged(): everything = jax.tree.map(lambda part: lax.all_gather(part, axis), value)]
    unnamed x6 -> x0, waiting for transfers between devices: 736 us -> none
    add x252 -> x0, other arithmetic: 138 us -> none  [the longest x126 135 us: softmax_join(): joined = out_a * factor_a[..., None] + out_b * factor_b[..., None]]
    pallas_call x0 -> x1, Pallas kernels: none -> 35.9 us  [body(): pl.pallas_call(kernel, out_shape=jax.ShapeDtypeStruct((STEPS, 1, 112), BF...]
  transfers between devices with their start and end apart: 4 -> 0, of which waited for: 2 -> 0; matrix products, arithmetic and copies ran while one was open for 4% -> 0% of each run, Pallas kernels for 0% -> 0%
where the time goes in v1:
time: 41.3 us; the launch traced here: 41 us
  Pallas kernels  35.9 us (87%)
  local copies, waits for them, and re-layouts  4.3 us (10%)
  between operations  0.76 us (2%)
    pallas_call x1, Pallas kernels, body(): pl.pallas_call(kernel, out_shape=jax.ShapeDtypeStruct((STEPS, 1, 112), BF...  35.9 us
    unnamed x10, local copies, waits for them, and re-layouts  3.79 us

profile of v1, /device:TPU:2, one launch (start us, length us, event | category | flops | bytes accessed | tf_op | source)
XLA Modules:
  0.0 41.0 jit_solution(1862165763886112265)
XLA Ops:
  0.0 0.0 copy-start.1
  0.0 0.0 copy-start
  0.0 0.0 copy-start.3
  0.0 0.0 copy-start.2
  0.7 0.7 %copy.10.new_rows = bf16[2,1,576]{2,1,0:T(2,128)(2,1)S(1)} copy(bf16[2,1,576]{2,0,1:T(2,128)(2,1)} %param.14) | data formatting | bytes 4608 | tf_op args[6]
  1.4 3.1 %copy.9.cache = bf16[1,2048,576]{2,1,0:T(8,128)(2,1)S(1)} copy(bf16[1,2048,576]{1,2,0:T(8,128)(2,1)} %param.13) | data formatting | bytes 4718592 | tf_op args[5]
  4.5 0.0 copy-done.1
  4.5 0.0 copy-done
  4.5 0.0 copy-done.3
  4.5 0.0 copy-done.2
  4.5 35.9 %shard_map.82 = bf16[2,1,112]{2,1,0:T(2,128)(2,1)S(1)} custom-call(bf16[2,1,2,128]{3,2,1,0:T(2,128)(2,1)S(1)} %copy-done.2, bf16[2,1,2,64]{3,2,1,0:T(2,128)(2,1)S(1)} %copy-done.3, bf16[2,128,512]{2,1,0:T(8,128)(2,1)S(1)} %copy-done, bf16[2,512,128]{2,1,0:T(8,128)(2,1)S(1)} %copy-done.1, bf16[256,7168]{1,0:T(8,128)(2,1)} %out_w.1, ...), custom_call_target="tpu_custom_call" | custom-call | tf_op jit(solution)/shard_map/pallas_call | solution.py:242
  40.5 0.5 %copy.11 = bf16[2,1,112]{2,0,1:T(2,128)(2,1)} copy(bf16[2,1,112]{2,1,0:T(2,128)(2,1)S(1)} %shard_map.82) | data formatting | bytes 896 | tf_op jit(solution)/shard_map/pallas_call | solution.py:242
Async XLA Ops:
  0.0 4.5 %copy-start.1 = (bf16[2,512,128]{2,1,0:T(8,128)(2,1)S(1)}, bf16[2,512,128]{2,1,0:T(8,128)(2,1)}, u32[]{:S(2)}) copy-start(bf16[2,512,128]{2,1,0:T(8,128)(2,1)} %uv.1) | copy-start | bytes 786436
  0.0 4.5 %copy-start = (bf16[2,128,512]{2,1,0:T(8,128)(2,1)S(1)}, bf16[2,128,512]{2,1,0:T(8,128)(2,1)}, u32[]{:S(2)}) copy-start(bf16[2,128,512]{2,1,0:T(8,128)(2,1)} %uk.1) | copy-start | bytes 786436
  0.0 4.5 %copy-start.3 = (bf16[2,1,2,64]{3,2,1,0:T(2,128)(2,1)S(1)}, bf16[2,1,2,64]{3,2,1,0:T(2,128)(2,1)}, u32[]{:S(2)}) copy-start(bf16[2,1,2,64]{3,2,1,0:T(2,128)(2,1)} %q_rope.1) | copy-start | bytes 1540
  0.0 4.5 %copy-start.2 = (bf16[2,1,2,128]{3,2,1,0:T(2,128)(2,1)S(1)}, bf16[2,1,2,128]{3,2,1,0:T(2,128)(2,1)}, u32[]{:S(2)}) copy-start(bf16[2,1,2,128]{3,2,1,0:T(2,128)(2,1)} %q_nope.1) | copy-start | bytes 3076

commit v2 on v1

--- a/solution.py
+++ b/solution.py
@@ -57,7 +57,7 @@
 
 def kernel(
     q_nope, q_rope, uk, uv, out_w, cache, new_rows, context, out,
-    qn_v, qr_v, uk_v, uv_v, w_v, c_v, new_v, ctx_s, qx, zq, q_all, keys, scores, ob, rb, rb2, ts, tr,
+    qn_v, qr_v, uk_v, uv_v, w_v, new_v, ctx_s, qx, zq, q_all, keys, scores, ob, rb, rb2, ts, tr,
     load_sem, send_sem, recv_sem,
 ):
     me = lax.axis_index("kv")
@@ -81,7 +81,7 @@
     loads = [
         pltpu.make_async_copy(src, dst, load_sem.at[k])
         for k, (src, dst) in enumerate(
-            [(q_nope, qn_v), (q_rope, qr_v), (uk, uk_v), (context, ctx_s), (new_rows, new_v), (cache.at[0], c_v), (uv, uv_v), (out_w, w_v)]
+            [(q_nope, qn_v), (q_rope, qr_v), (uk, uk_v), (context, ctx_s), (new_rows, new_v), (cache.at[0], keys.at[pl.ds(0, WIDE)]), (uv, uv_v), (out_w, w_v)]
         )
     ]
     for load in loads:
@@ -133,16 +133,19 @@
     l_new.wait()
     l_cache.wait()
     length = ctx_s[0]
+    rows = jnp.concatenate([new_v[0].astype(F32), jnp.zeros((STEPS, WIDE_PAD - WIDE), F32)], axis=1)
+    appended = jnp.concatenate([rows, jnp.zeros((8 - STEPS, WIDE_PAD), F32)], axis=0).T
+    row = lax.broadcasted_iota(jnp.int32, (WIDE_PAD - WIDE, 1), 0)
 
     def prepare(k, _):
-        base = pl.multiple_of(k * 256, 256)
-        token = (lax.broadcasted_iota(jnp.int32, (256, 1), 0) + base) * 64 + me
-        block = c_v[pl.ds(base, 256), :].astype(F32)
+        here = pl.ds(pl.multiple_of(k * 256, 256), 256)
+        token = (lax.broadcasted_iota(jnp.int32, (1, 256), 1) + k * 256) * 64 + me
+        block = keys[0:WIDE, here].astype(F32)
         for step in range(STEPS):
-            block = jnp.where(token == length + step, new_v[step].astype(F32), block)
-        lane = lax.broadcasted_iota(jnp.int32, (256, WIDE_PAD - WIDE), 1)
-        mask = jnp.where((lane < STEPS) & (token > length + lane), NEVER, 0.0)
-        keys[pl.ds(base, 256), :] = jnp.concatenate([block, mask], axis=1).astype(BF16)
+            block = jnp.where(token == length + step, appended[0:WIDE, step : step + 1], block)
+        keys[0:WIDE, here] = block.astype(BF16)
+        mask = jnp.where((row < STEPS) & (token > length + row), NEVER, 0.0)
+        keys[WIDE:, here] = mask.astype(BF16)
         return 0
 
     lax.fori_loop(0, 4, prepare, 0)
@@ -159,9 +162,7 @@
     queries = q_all[...]
     peak = None
     for k in range(4):
-        part = lax.dot_general(
-            queries, keys[k * 512 : k * 512 + 512, :], (((1,), (1,)), ((), ())), preferred_element_type=F32
-        )
+        part = jnp.dot(queries, keys[:, k * 512 : k * 512 + 512], preferred_element_type=F32)
         scores[:, k * 512 : k * 512 + 512] = part
         for j in range(4):
             tile = part[:, j * 128 : j * 128 + 128]
@@ -174,8 +175,8 @@
         expo = jnp.exp2(scores[:, k * 512 : k * 512 + 512] * scale - peak)
         for j in range(4):
             total = total + expo[:, j * 128 : j * 128 + 128]
-        value = value + jnp.dot(
-            expo.astype(BF16), keys[k * 512 : k * 512 + 512, 0:LAT], preferred_element_type=F32
+        value = value + lax.dot_general(
+            expo.astype(BF16), keys[0:LAT, k * 512 : k * 512 + 512], (((1,), (1,)), ((), ())), preferred_element_type=F32
         )
     ob[:, 0:LAT] = value.astype(BF16)
     ob[:, LAT:] = with_stats(peak, jnp.sum(total, axis=1, keepdims=True), 256).astype(BF16)
@@ -228,7 +229,7 @@
                 remote(ts.at[peer, pl.ds(0, 2)], tr.at[me, pl.ds(0, 2)], 4, {"kv": peer})
     take(tr.at[pl.ds(0, 63), pl.ds(0, 2)], recv_sem.at[4])
     result = jnp.sum(tr[:, 0:2, :], axis=0)
-    out[:, 0, :] = result[:, 0:112].astype(BF16)
+    out[0] = result[:, 0:112].astype(BF16)
 
     take(zq.at[pl.ds(0, 3), pl.ds(0, 4)], send_sem.at[0])
     take(q_all.at[pl.ds(0, 240)], send_sem.at[1])
@@ -237,12 +238,12 @@
     take(ts.at[pl.ds(0, 63), pl.ds(0, 2)], send_sem.at[4])
 
 
-def body(*args):
-    any_space = pl.BlockSpec(memory_space=pl.ANY)
-    return pl.pallas_call(
+def body(q_nope, q_rope, uk, uv, out_w, cache, new_rows, context):
+    hbm = pl.BlockSpec(memory_space=pltpu.HBM)
+    result = pl.pallas_call(
         kernel,
-        out_shape=jax.ShapeDtypeStruct((STEPS, 1, 112), BF16),
-        in_specs=[any_space] * 8,
+        out_shape=pltpu.VMEM((1, STEPS, 112), BF16),
+        in_specs=[hbm] * 8,
         out_specs=pl.BlockSpec(memory_space=pltpu.VMEM),
         scratch_shapes=[
             pltpu.VMEM((2, 1, 2, 128), BF16),
@@ -250,13 +251,12 @@
             pltpu.VMEM((2, 128, LAT), BF16),
             pltpu.VMEM((2, LAT, 128), BF16),
             pltpu.VMEM((256, 7168), BF16),
-            pltpu.VMEM((2048, WIDE), BF16),
-            pltpu.VMEM((2, 1, WIDE), BF16),
+            pltpu.VMEM((1, 2, WIDE), BF16),
             pltpu.SMEM((1,), jnp.int32),
             pltpu.VMEM((8, 128), F32),
             pltpu.VMEM((4, 8, WIDE_PAD), F32),
             pltpu.VMEM((256, WIDE_PAD), BF16),
-            pltpu.VMEM((2048, WIDE_PAD), BF16),
+            pltpu.VMEM((WIDE_PAD, 2048), BF16),
             pltpu.VMEM((256, 2048), F32),
             pltpu.VMEM((256, WIDE_PAD), BF16),
             pltpu.VMEM((256, WIDE_PAD), BF16),
@@ -268,9 +268,10 @@
             pltpu.SemaphoreType.DMA((5,)),
         ],
         compiler_params=pltpu.CompilerParams(
-            collective_id=0, has_side_effects=True, vmem_limit_bytes=48 << 20
+            collective_id=0, has_side_effects=True, vmem_limit_bytes=60 << 20
         ),
-    )(*args)
+    )(q_nope, q_rope, uk, uv, out_w, jnp.swapaxes(cache, 1, 2), jnp.swapaxes(new_rows, 0, 1), context)
+    return jnp.swapaxes(result, 0, 1)
 
 
 def solution(mesh):

time: 41.3 us -> 37.3 us (0.903)
  local copies, waits for them, and re-layouts: 4.3 us -> 0.51 us
    unnamed x10 -> x1, local copies, waits for them, and re-layouts: 3.79 us -> 0.51 us
    pallas_call x1 -> x0, local copies, waits for them, and re-layouts: 0.51 us -> none  [body(): pl.pallas_call(kernel, out_shape=jax.ShapeDtypeStruct((STEPS, 1, 112), BF...]
where the time goes in v2:
time: 37.3 us; the launch traced here: 37.1 us
  Pallas kernels  35.9 us (96%)
  between operations  0.66 us (2%)
  local copies, waits for them, and re-layouts  0.51 us (1%)
    pallas_call x1, Pallas kernels, body(): pl.pallas_call(kernel, out_shape=pltpu.VMEM((1, STEPS, 112), BF16), in_sp...  35.9 us

profile of v2, /device:TPU:2, one launch (start us, length us, event | category | flops | bytes accessed | tf_op | source)
XLA Modules:
  0.0 37.1 jit_solution(10975998981493868980)
XLA Ops:
  0.7 35.9 %shard_map.82 = bf16[1,2,112]{2,1,0:T(2,128)(2,1)S(1)} custom-call(bf16[2,1,2,128]{3,2,1,0:T(2,128)(2,1)} %q_nope.1, bf16[2,1,2,64]{3,2,1,0:T(2,128)(2,1)} %q_rope.1, bf16[2,128,512]{2,1,0:T(8,128)(2,1)} %uk.1, bf16[2,512,128]{2,1,0:T(8,128)(2,1)} %uv.1, bf16[256,7168]{1,0:T(8,128)(2,1)} %out_w.1, bf16[1,576,2048]{2,1,0:T(8,128)(2,1)} %bitcast.4, ...), custom_call_target="tpu_custom_call" | custom-call | tf_op jit(solution)/shard_map/pallas_call | solution.py:243
  36.6 0.5 %copy.10 = bf16[2,1,112]{2,0,1:T(2,128)(2,1)} copy(bf16[2,1,112]{2,0,1:T(2,128)(2,1)S(1)} %bitcast.3) | data formatting | bytes 896

commit v3 on v2

--- a/solution.py
+++ b/solution.py
@@ -21,6 +21,7 @@
 WIDE = LAT + ROPE
 WIDE_PAD = 640
 NEVER = -1e30
+SENT = 18
 
 RING = [(dy, dx) for dy in range(SIDE) for dx in range(SIDE) if dy or dx]
 RING.sort(key=lambda d: -(min(d[0], SIDE - d[0]) + min(d[1], SIDE - d[1])))
@@ -34,30 +35,16 @@
 
 def with_stats(peak, total, rows):
     lane = lax.broadcasted_iota(jnp.int32, (rows, 128), 1)
+    row = lax.broadcasted_iota(jnp.int32, (rows, 128), 0) % ROWS
     result = jnp.zeros((rows, 128), F32)
     for at, part in enumerate((*split(peak), *split(total))):
-        result = jnp.where(lane == at, part, result)
+        result = jnp.where(lane == row + at * ROWS, part, result)
     return result
-
-
-def join(parts, pick, out_rows):
-    stats = parts[:, LAT:].astype(F32).T
-    peak = stats[0:1] + stats[1:2]
-    total = stats[2:3] + stats[3:4]
-    n = parts.shape[0]
-    peaks = jnp.where(pick, jnp.broadcast_to(peak, (out_rows, n)), -3e38)
-    top = jnp.max(peaks, axis=1, keepdims=True)
-    factor = jnp.where(pick, jnp.exp2(peaks - top), 0.0)
-    whole = jnp.sum(factor * total, axis=1, keepdims=True)
-    high, low = split(factor)
-    both = jnp.concatenate([high, low], axis=0).astype(BF16)
-    summed = jnp.dot(both, parts[:, :LAT], preferred_element_type=F32)
-    return summed[:out_rows] + summed[out_rows:], top, whole
 
 
 def kernel(
     q_nope, q_rope, uk, uv, out_w, cache, new_rows, context, out,
-    qn_v, qr_v, uk_v, uv_v, w_v, new_v, ctx_s, qx, zq, q_all, keys, scores, ob, rb, rb2, ts, tr,
+    qn_v, qr_v, uk_v, uv_v, w_v, new_v, ctx_s, qx, zq, q_all, keys, scores, vals, stats, ob, rb, spread, ts, tr,
     load_sem, send_sem, recv_sem,
 ):
     me = lax.axis_index("kv")
@@ -156,6 +143,9 @@
     for peer in in_plane:
         remote(mine, mine, 1, plane_id(peer))
     lax.fori_loop(4, 8, prepare, 0)
+    column = lax.broadcasted_iota(jnp.int32, (128, 1024), 1) // 16
+    place = lax.broadcasted_iota(jnp.int32, (128, 1024), 0)
+    spread[...] = jnp.where(column == place, 1.0, 0.0).astype(BF16)
     take(q_all.at[pl.ds(0, 240)], recv_sem.at[1])
 
     scale = math.log2(math.e) * (128 + ROPE) ** -0.5
@@ -178,32 +168,61 @@
         value = value + lax.dot_general(
             expo.astype(BF16), keys[0:LAT, k * 512 : k * 512 + 512], (((1,), (1,)), ((), ())), preferred_element_type=F32
         )
-    ob[:, 0:LAT] = value.astype(BF16)
-    ob[:, LAT:] = with_stats(peak, jnp.sum(total, axis=1, keepdims=True), 256).astype(BF16)
-
-    mine = pl.ds(pl.multiple_of(plane * 16, 16), 16)
-    for peer in in_plane:
-        theirs = pl.ds(pl.multiple_of((peer[0] * 4 + peer[1]) * 16, 16), 16)
-        remote(ob.at[theirs], rb.at[mine], 2, plane_id(peer))
-    rb[mine, :] = ob[mine, :]
-    take(rb.at[pl.ds(0, 240)], recv_sem.at[2])
-    pick = (
-        lax.broadcasted_iota(jnp.int32, (16, 256), 1) % 16
-        == lax.broadcasted_iota(jnp.int32, (16, 256), 0)
-    )
-    summed, top, whole = join(rb[...], pick, 16)
-    mine = rb2.at[pl.ds(pl.multiple_of(z * 16, 16), 16)]
-    mine[...] = jnp.concatenate([summed, with_stats(top, whole, 16)], axis=1).astype(BF16)
-    for peer in in_line:
-        remote(mine, mine, 3, line_id(peer))
+    vals[...] = value
+    stats[...] = with_stats(peak, jnp.sum(total, axis=1, keepdims=True), 256)
+
+    low_half = lax.broadcasted_iota(jnp.int32, (8, 1), 0) < 4
+
+    def halves(left, right):
+        return (
+            jnp.where(low_half, left, pltpu.roll(right, 4, 0)),
+            jnp.where(low_half, pltpu.roll(left, 4, 0), right),
+        )
+
+    own_pair = z // 2
+    for z_pair in (1 - own_pair, own_pair):
+        for dy, dx in (*RING, (0, 0)):
+            to_y, to_x = (y + dy) % 4, (x + dx) % 4
+            eight = pl.ds(pl.multiple_of(((to_y * 4 + to_x) * 2 + z_pair) * 8, 8), 8)
+            quarters = [vals[eight, k * 128 : k * 128 + 128] for k in range(4)]
+            first, second = zip(halves(*quarters[:2]), halves(*quarters[2:]))
+            note = stats[eight, :]
+            note = note + pltpu.roll(note, 1, 0)
+            note = note + pltpu.roll(note, 2, 0)
+            for j, (rows, shift) in enumerate(((first, 5), (second, 1))):
+                peer = to_y * 16 + (z_pair * 2 + j) * 4 + to_x
+                ob[peer, 0:16, :] = jnp.concatenate(rows, axis=0).astype(BF16)
+                moved = pltpu.roll(note, shift, 0)
+                ob[peer, 16:32, :] = jnp.concatenate([moved, moved], axis=0).astype(BF16)
+            for j in (1, 0):
+                peer = to_y * 16 + (z_pair * 2 + (z + j) % 2) * 4 + to_x
+                if z_pair is own_pair and dy == 0 and dx == 0 and j == 0:
+                    rb[me] = ob[me]
+                else:
+                    remote(ob.at[peer, pl.ds(0, SENT)], rb.at[me, pl.ds(0, SENT)], 2, {"kv": peer})
     l_uv.wait()
     l_w.wait()
-    take(rb2.at[pl.ds(0, 48)], recv_sem.at[3])
-    pick = lax.broadcasted_iota(jnp.int32, (8, 64), 1) % 16 == z * 4 + (
-        lax.broadcasted_iota(jnp.int32, (8, 64), 0) % 4
+    take(rb.at[pl.ds(0, 63), pl.ds(0, SENT)], recv_sem.at[2])
+    notes = jnp.concatenate(
+        [rb[k, 16:18, :].astype(F32)[0:1] for k in range(64)] + [jnp.zeros((64, 128), F32)], axis=0
+    ).T
+    known = lax.broadcasted_iota(jnp.int32, (ROWS, 128), 1) < 64
+    peak = jnp.where(known, notes[0:4] + notes[4:8], -3e38)
+    factor = jnp.where(known, jnp.exp2(peak - jnp.max(peak, axis=1, keepdims=True)), 0.0)
+    whole = jnp.sum(factor * (notes[8:12] + notes[12:16]), axis=1, keepdims=True)
+    factor = factor / whole
+    factor = jnp.concatenate([factor, factor], axis=0).astype(BF16)
+    factor = jnp.dot(factor, spread[...], preferred_element_type=F32)
+    column = lax.broadcasted_iota(jnp.int32, (16, 1024), 1) % 16
+    place = lax.broadcasted_iota(jnp.int32, (16, 1024), 0)
+    factor = jnp.where(column == place, jnp.concatenate([factor, factor], axis=0), 0.0).astype(BF16)
+    joined = jnp.dot(
+        factor, rb[:, 0:16, :].reshape(1024, 128), preferred_element_type=F32
     )
-    summed, top, whole = join(rb2[...], pick, 8)
-    latent = (summed / whole).astype(BF16)
+    top, bottom = joined[0:8], joined[8:16]
+    latent = jnp.concatenate(
+        [top, pltpu.roll(top, 4, 0), bottom, pltpu.roll(bottom, 4, 0)], axis=1
+    ).astype(BF16)
 
     head_value = jnp.concatenate(
         [
@@ -226,16 +245,15 @@
             if i == 0 and j == 0:
                 tr[me, 0:2, :] = ts[me, 0:2, :]
             else:
-                remote(ts.at[peer, pl.ds(0, 2)], tr.at[me, pl.ds(0, 2)], 4, {"kv": peer})
-    take(tr.at[pl.ds(0, 63), pl.ds(0, 2)], recv_sem.at[4])
+                remote(ts.at[peer, pl.ds(0, 2)], tr.at[me, pl.ds(0, 2)], 3, {"kv": peer})
+    take(tr.at[pl.ds(0, 63), pl.ds(0, 2)], recv_sem.at[3])
     result = jnp.sum(tr[:, 0:2, :], axis=0)
     out[0] = result[:, 0:112].astype(BF16)
 
     take(zq.at[pl.ds(0, 3), pl.ds(0, 4)], send_sem.at[0])
     take(q_all.at[pl.ds(0, 240)], send_sem.at[1])
-    take(ob.at[pl.ds(0, 240)], send_sem.at[2])
-    take(rb2.at[pl.ds(0, 48)], send_sem.at[3])
-    take(ts.at[pl.ds(0, 63), pl.ds(0, 2)], send_sem.at[4])
+    take(ob.at[pl.ds(0, 63), pl.ds(0, SENT)], send_sem.at[2])
+    take(ts.at[pl.ds(0, 63), pl.ds(0, 2)], send_sem.at[3])
 
 
 def body(q_nope, q_rope, uk, uv, out_w, cache, new_rows, context):
@@ -258,14 +276,16 @@
             pltpu.VMEM((256, WIDE_PAD), BF16),
             pltpu.VMEM((WIDE_PAD, 2048), BF16),
             pltpu.VMEM((256, 2048), F32),
-            pltpu.VMEM((256, WIDE_PAD), BF16),
-            pltpu.VMEM((256, WIDE_PAD), BF16),
-            pltpu.VMEM((64, WIDE_PAD), BF16),
+            pltpu.VMEM((256, LAT), F32),
+            pltpu.VMEM((256, 128), F32),
+            pltpu.VMEM((64, 32, 128), BF16),
+            pltpu.VMEM((64, 32, 128), BF16),
+            pltpu.VMEM((128, 1024), BF16),
             pltpu.VMEM((64, 8, 128), F32),
             pltpu.VMEM((64, 8, 128), F32),
             pltpu.SemaphoreType.DMA((8,)),
-            pltpu.SemaphoreType.DMA((5,)),
-            pltpu.SemaphoreType.DMA((5,)),
+            pltpu.SemaphoreType.DMA((4,)),
+            pltpu.SemaphoreType.DMA((4,)),
         ],
         compiler_params=pltpu.CompilerParams(
             collective_id=0, has_side_effects=True, vmem_limit_bytes=60 << 20

time: 37.3 us -> 35.5 us (0.952)
  Pallas kernels: 35.9 us -> 33.9 us
    pallas_call x1, Pallas kernels: 35.9 us -> 33.9 us  [body(): pl.pallas_call(kernel, out_shape=pltpu.VMEM((1, STEPS, 112), BF16), in_sp...]
where the time goes in v3:
time: 35.5 us; the launch traced here: 35.1 us
  Pallas kernels  33.9 us (95%)
  between operations  0.66 us (2%)
  local copies, waits for them, and re-layouts  0.51 us (1%)
    pallas_call x1, Pallas kernels, body(): pl.pallas_call(kernel, out_shape=pltpu.VMEM((1, STEPS, 112), BF16), in_sp...  33.9 us

profile of v3, /device:TPU:2, one launch (start us, length us, event | category | flops | bytes accessed | tf_op | source)
XLA Modules:
  0.0 35.1 jit_solution(285253442256863701)
XLA Ops:
  0.7 33.9 %shard_map.82 = bf16[1,2,112]{2,1,0:T(2,128)(2,1)S(1)} custom-call(bf16[2,1,2,128]{3,2,1,0:T(2,128)(2,1)} %q_nope.1, bf16[2,1,2,64]{3,2,1,0:T(2,128)(2,1)} %q_rope.1, bf16[2,128,512]{2,1,0:T(8,128)(2,1)} %uk.1, bf16[2,512,128]{2,1,0:T(8,128)(2,1)} %uv.1, bf16[256,7168]{1,0:T(8,128)(2,1)} %out_w.1, bf16[1,576,2048]{2,1,0:T(8,128)(2,1)} %bitcast.4, ...), custom_call_target="tpu_custom_call" | custom-call | tf_op jit(solution)/shard_map/pallas_call | solution.py:261
  34.6 0.5 %copy.10 = bf16[2,1,112]{2,0,1:T(2,128)(2,1)} copy(bf16[2,1,112]{2,0,1:T(2,128)(2,1)S(1)} %bitcast.3) | data formatting | bytes 896

commit v4 on v3

--- a/solution.py
+++ b/solution.py
@@ -44,7 +44,7 @@
 
 def kernel(
     q_nope, q_rope, uk, uv, out_w, cache, new_rows, context, out,
-    qn_v, qr_v, uk_v, uv_v, w_v, new_v, ctx_s, qx, zq, q_all, keys, scores, vals, stats, ob, rb, spread, ts, tr,
+    qn_v, qr_v, uk_v, uv_v, w_v, new_v, ctx_v, qx, zq, q_all, keys, latents, scores, vals, stats, ob, rb, spread, ts, tr,
     load_sem, send_sem, recv_sem,
 ):
     me = lax.axis_index("kv")
@@ -59,19 +59,22 @@
     def line_id(peer):
         return {"kv": y * 16 + peer * 4 + x}
 
+    loads = [
+        pltpu.make_async_copy(src, dst, load_sem.at[k])
+        for k, (src, dst) in enumerate(
+            [(q_nope, qn_v), (q_rope, qr_v), (uk, uk_v), (context, ctx_v), (new_rows, new_v), (cache.at[0], keys.at[pl.ds(0, WIDE)]), (uv, uv_v), (out_w, w_v)]
+        )
+    ]
     barrier = pltpu.get_barrier_semaphore()
-    for peer in in_plane:
+    for peer in in_plane[:5]:
         pl.semaphore_signal(barrier, inc=1, device_id=plane_id(peer), device_id_type=MESH)
     for peer in in_line:
         pl.semaphore_signal(barrier, inc=1, device_id=line_id(peer), device_id_type=MESH)
-
-    loads = [
-        pltpu.make_async_copy(src, dst, load_sem.at[k])
-        for k, (src, dst) in enumerate(
-            [(q_nope, qn_v), (q_rope, qr_v), (uk, uk_v), (context, ctx_s), (new_rows, new_v), (cache.at[0], keys.at[pl.ds(0, WIDE)]), (uv, uv_v), (out_w, w_v)]
-        )
-    ]
-    for load in loads:
+    for peer in in_plane[5:]:
+        pl.semaphore_signal(barrier, inc=1, device_id=plane_id(peer), device_id_type=MESH)
+    for load in loads[:3]:
+        load.start()
+    for load in loads[3:]:
         load.start()
     l_qn, l_qr, l_uk, l_ctx, l_new, l_cache, l_uv, l_w = loads
 
@@ -119,7 +122,7 @@
     l_ctx.wait()
     l_new.wait()
     l_cache.wait()
-    length = ctx_s[0]
+    length = ctx_v[...]
     rows = jnp.concatenate([new_v[0].astype(F32), jnp.zeros((STEPS, WIDE_PAD - WIDE), F32)], axis=1)
     appended = jnp.concatenate([rows, jnp.zeros((8 - STEPS, WIDE_PAD), F32)], axis=0).T
     row = lax.broadcasted_iota(jnp.int32, (WIDE_PAD - WIDE, 1), 0)
@@ -131,6 +134,7 @@
         for step in range(STEPS):
             block = jnp.where(token == length + step, appended[0:WIDE, step : step + 1], block)
         keys[0:WIDE, here] = block.astype(BF16)
+        latents[here, :] = block[0:LAT].astype(BF16).T
         mask = jnp.where((row < STEPS) & (token > length + row), NEVER, 0.0)
         keys[WIDE:, here] = mask.astype(BF16)
         return 0
@@ -149,27 +153,32 @@
     take(q_all.at[pl.ds(0, 240)], recv_sem.at[1])
 
     scale = math.log2(math.e) * (128 + ROPE) ** -0.5
-    queries = q_all[...]
-    peak = None
-    for k in range(4):
-        part = jnp.dot(queries, keys[:, k * 512 : k * 512 + 512], preferred_element_type=F32)
-        scores[:, k * 512 : k * 512 + 512] = part
-        for j in range(4):
-            tile = part[:, j * 128 : j * 128 + 128]
-            peak = tile if peak is None else jnp.maximum(peak, tile)
-    high, low = split(jnp.max(peak, axis=1, keepdims=True) * scale)
-    peak = high + low
-    total = jnp.zeros((256, 128), F32)
-    value = jnp.zeros((256, LAT), F32)
-    for k in range(4):
-        expo = jnp.exp2(scores[:, k * 512 : k * 512 + 512] * scale - peak)
-        for j in range(4):
-            total = total + expo[:, j * 128 : j * 128 + 128]
-        value = value + lax.dot_general(
-            expo.astype(BF16), keys[0:LAT, k * 512 : k * 512 + 512], (((1,), (1,)), ((), ())), preferred_element_type=F32
-        )
-    vals[...] = value
-    stats[...] = with_stats(peak, jnp.sum(total, axis=1, keepdims=True), 256)
+
+    def attend(part):
+        blocks = [pl.ds(pl.multiple_of(to_y * 64, 64), 64) for to_y in part]
+        queries = jnp.concatenate([q_all[block, :] for block in blocks], axis=0)
+        peak = None
+        for k in range(4):
+            tiles = jnp.dot(queries, keys[:, k * 512 : k * 512 + 512], preferred_element_type=F32)
+            scores[:, k * 512 : k * 512 + 512] = tiles
+            for j in range(4):
+                tile = tiles[:, j * 128 : j * 128 + 128]
+                peak = tile if peak is None else jnp.maximum(peak, tile)
+        high, low = split(jnp.max(peak, axis=1, keepdims=True) * scale)
+        peak = high + low
+        total = jnp.zeros((128, 128), F32)
+        value = jnp.zeros((128, LAT), F32)
+        for k in range(4):
+            expo = jnp.exp2(scores[:, k * 512 : k * 512 + 512] * scale - peak)
+            for j in range(4):
+                total = total + expo[:, j * 128 : j * 128 + 128]
+            value = value + jnp.dot(
+                expo.astype(BF16), latents[k * 512 : k * 512 + 512, :], preferred_element_type=F32
+            )
+        note = with_stats(peak, jnp.sum(total, axis=1, keepdims=True), 128)
+        for k, block in enumerate(blocks):
+            vals[block, :] = value[k * 64 : k * 64 + 64]
+            stats[block, :] = note[k * 64 : k * 64 + 64]
 
     low_half = lax.broadcasted_iota(jnp.int32, (8, 1), 0) < 4
 
@@ -180,26 +189,37 @@
         )
 
     own_pair = z // 2
-    for z_pair in (1 - own_pair, own_pair):
-        for dy, dx in (*RING, (0, 0)):
-            to_y, to_x = (y + dy) % 4, (x + dx) % 4
-            eight = pl.ds(pl.multiple_of(((to_y * 4 + to_x) * 2 + z_pair) * 8, 8), 8)
-            quarters = [vals[eight, k * 128 : k * 128 + 128] for k in range(4)]
-            first, second = zip(halves(*quarters[:2]), halves(*quarters[2:]))
-            note = stats[eight, :]
-            note = note + pltpu.roll(note, 1, 0)
-            note = note + pltpu.roll(note, 2, 0)
-            for j, (rows, shift) in enumerate(((first, 5), (second, 1))):
-                peer = to_y * 16 + (z_pair * 2 + j) * 4 + to_x
-                ob[peer, 0:16, :] = jnp.concatenate(rows, axis=0).astype(BF16)
-                moved = pltpu.roll(note, shift, 0)
-                ob[peer, 16:32, :] = jnp.concatenate([moved, moved], axis=0).astype(BF16)
-            for j in (1, 0):
-                peer = to_y * 16 + (z_pair * 2 + (z + j) % 2) * 4 + to_x
-                if z_pair is own_pair and dy == 0 and dx == 0 and j == 0:
-                    rb[me] = ob[me]
-                else:
-                    remote(ob.at[peer, pl.ds(0, SENT)], rb.at[me, pl.ds(0, SENT)], 2, {"kv": peer})
+
+    def deliver(part, z_pair, last=False):
+        for dy, to_y in enumerate(part):
+            for dx in (2, 1, 3, 0):
+                to_x = (x + dx) % 4
+                eight = pl.ds(pl.multiple_of(((to_y * 4 + to_x) * 2 + z_pair) * 8, 8), 8)
+                quarters = [vals[eight, k * 128 : k * 128 + 128] for k in range(4)]
+                first, second = zip(halves(*quarters[:2]), halves(*quarters[2:]))
+                note = stats[eight, :]
+                note = note + pltpu.roll(note, 1, 0)
+                note = note + pltpu.roll(note, 2, 0)
+                for j, (rows, shift) in enumerate(((first, 5), (second, 1))):
+                    peer = to_y * 16 + (z_pair * 2 + j) * 4 + to_x
+                    ob[peer, 0:16, :] = jnp.concatenate(rows, axis=0).astype(BF16)
+                    moved = pltpu.roll(note, shift, 0)
+                    ob[peer, 16:32, :] = jnp.concatenate([moved, moved], axis=0).astype(BF16)
+                for j in (1, 0):
+                    peer = to_y * 16 + (z_pair * 2 + (z + j) % 2) * 4 + to_x
+                    if last and dy == 1 and dx == 0 and j == 0:
+                        rb[me] = ob[me]
+                    else:
+                        remote(ob.at[peer, pl.ds(0, SENT)], rb.at[me, pl.ds(0, SENT)], 2, {"kv": peer})
+
+    far = ((y + 2) % 4, (y + 3) % 4)
+    near = ((y + 1) % 4, y)
+    attend(far)
+    deliver(far, 1 - own_pair)
+    attend(near)
+    deliver(near, 1 - own_pair)
+    deliver(far, own_pair)
+    deliver(near, own_pair, last=True)
     l_uv.wait()
     l_w.wait()
     take(rb.at[pl.ds(0, 63), pl.ds(0, SENT)], recv_sem.at[2])
@@ -234,18 +254,20 @@
     pairs = head_value + pltpu.roll(head_value, 7, 0)
     first = lax.broadcasted_iota(jnp.int32, (8, 1), 0) == 0
     flat = jnp.where(first, pairs, pltpu.roll(pairs, 7, 0)).astype(BF16)
-    for i in (4, 3, 5, 2, 6, 1, 7, 0):
-        group = (me // 8 + i) % 8
-        columns = pl.ds(pl.multiple_of(group * 896, 128), 896)
-        term = jnp.dot(flat, w_v[:, columns], preferred_element_type=F32)
-        for j in range(8):
-            ts[group * 8 + j, :, 0:112] = term[:, j * 112 : j * 112 + 112]
-        for j in range(8):
-            peer = group * 8 + (me + j) % 8
-            if i == 0 and j == 0:
-                tr[me, 0:2, :] = ts[me, 0:2, :]
-            else:
-                remote(ts.at[peer, pl.ds(0, 2)], tr.at[me, pl.ds(0, 2)], 3, {"kv": peer})
+    for z_pair in (1 - own_pair, own_pair):
+        for dy in (2, 1, 3, 0):
+            group = ((y + dy) % 4) * 2 + z_pair
+            columns = pl.ds(pl.multiple_of(group * 896, 128), 896)
+            term = jnp.dot(flat, w_v[:, columns], preferred_element_type=F32)
+            for j in range(8):
+                ts[group * 8 + j, :, 0:112] = term[:, j * 112 : j * 112 + 112]
+            for dx in (2, 1, 3, 0):
+                for dz in (1, 0):
+                    peer = group * 8 + ((z + dz) % 2) * 4 + (x + dx) % 4
+                    if z_pair is own_pair and dy == 0 and dx == 0 and dz == 0:
+                        tr[me, 0:2, :] = ts[me, 0:2, :]
+                    else:
+                        remote(ts.at[peer, pl.ds(0, 2)], tr.at[me, pl.ds(0, 2)], 3, {"kv": peer})
     take(tr.at[pl.ds(0, 63), pl.ds(0, 2)], recv_sem.at[3])
     result = jnp.sum(tr[:, 0:2, :], axis=0)
     out[0] = result[:, 0:112].astype(BF16)
@@ -270,12 +292,13 @@
             pltpu.VMEM((2, LAT, 128), BF16),
             pltpu.VMEM((256, 7168), BF16),
             pltpu.VMEM((1, 2, WIDE), BF16),
-            pltpu.SMEM((1,), jnp.int32),
+            pltpu.VMEM((1, 1), jnp.int32),
             pltpu.VMEM((8, 128), F32),
             pltpu.VMEM((4, 8, WIDE_PAD), F32),
             pltpu.VMEM((256, WIDE_PAD), BF16),
             pltpu.VMEM((WIDE_PAD, 2048), BF16),
-            pltpu.VMEM((256, 2048), F32),
+            pltpu.VMEM((2048, LAT), BF16),
+            pltpu.VMEM((128, 2048), F32),
             pltpu.VMEM((256, LAT), F32),
             pltpu.VMEM((256, 128), F32),
             pltpu.VMEM((64, 32, 128), BF16),
@@ -290,7 +313,7 @@
         compiler_params=pltpu.CompilerParams(
             collective_id=0, has_side_effects=True, vmem_limit_bytes=60 << 20
         ),
-    )(q_nope, q_rope, uk, uv, out_w, jnp.swapaxes(cache, 1, 2), jnp.swapaxes(new_rows, 0, 1), context)
+    )(q_nope, q_rope, uk, uv, out_w, jnp.swapaxes(cache, 1, 2), jnp.swapaxes(new_rows, 0, 1), context.reshape(1, 1))
     return jnp.swapaxes(result, 0, 1)
 
 

time: 35.5 us -> 34.2 us (0.963)
  Pallas kernels: 33.9 us -> 32.7 us
    pallas_call x1, Pallas kernels: 33.9 us -> 32.7 us  [body(): pl.pallas_call(kernel, out_shape=pltpu.VMEM((1, STEPS, 112), BF16), in_sp...]
where the time goes in v4:
time: 34.2 us; the launch traced here: 33.9 us
  Pallas kernels  32.7 us (96%)
  between operations  0.66 us (2%)
  local copies, waits for them, and re-layouts  0.51 us (1%)
    pallas_call x1, Pallas kernels, body(): pl.pallas_call(kernel, out_shape=pltpu.VMEM((1, STEPS, 112), BF16), in_sp...  32.7 us

profile of v4, /device:TPU:2, one launch (start us, length us, event | category | flops | bytes accessed | tf_op | source)
XLA Modules:
  0.0 33.9 jit_solution(5389114628483091203)
XLA Ops:
  0.7 32.7 %shard_map.82 = bf16[1,2,112]{2,1,0:T(2,128)(2,1)S(1)} custom-call(bf16[2,1,2,128]{3,2,1,0:T(2,128)(2,1)} %q_nope.1, bf16[2,1,2,64]{3,2,1,0:T(2,128)(2,1)} %q_rope.1, bf16[2,128,512]{2,1,0:T(8,128)(2,1)} %uk.1, bf16[2,512,128]{2,1,0:T(8,128)(2,1)} %uv.1, bf16[256,7168]{1,0:T(8,128)(2,1)} %out_w.1, bf16[1,576,2048]{2,1,0:T(8,128)(2,1)} %bitcast.6, ...), custom_call_target="tpu_custom_call" | custom-call | tf_op jit(solution)/shard_map/pallas_call | solution.py:283
  33.4 0.5 %copy.10 = bf16[2,1,112]{2,0,1:T(2,128)(2,1)} copy(bf16[2,1,112]{2,0,1:T(2,128)(2,1)S(1)} %bitcast.5) | data formatting | bytes 896

commit v5 on v4

--- a/solution.py
+++ b/solution.py
@@ -21,11 +21,11 @@
 WIDE = LAT + ROPE
 WIDE_PAD = 640
 NEVER = -1e30
+ASKED = 20
 SENT = 18
 
 RING = [(dy, dx) for dy in range(SIDE) for dx in range(SIDE) if dy or dx]
 RING.sort(key=lambda d: -(min(d[0], SIDE - d[0]) + min(d[1], SIDE - d[1])))
-LINE = (3, 2, 1)
 
 
 def split(value):
@@ -44,14 +44,14 @@
 
 def kernel(
     q_nope, q_rope, uk, uv, out_w, cache, new_rows, context, out,
-    qn_v, qr_v, uk_v, uv_v, w_v, new_v, ctx_v, qx, zq, q_all, keys, latents, scores, vals, stats, ob, rb, spread, ts, tr,
+    qn_v, qr_v, uk_v, uv_v, w_v, new_v, ctx_v, qx, qs, q_all, keys, latents, scores, vals, stats, ob, rb, spread, ts, tr,
     load_sem, send_sem, recv_sem,
 ):
     me = lax.axis_index("kv")
     y, z, x = me // 16, (me // 4) % 4, me % 4
-    plane = y * 4 + x
     in_plane = [((y + dy) % 4, (x + dx) % 4) for dy, dx in RING]
-    in_line = [(z + dz) % 4 for dz in LINE]
+    own_pair = z // 2
+    in_line = [3 - 3 * own_pair, 2 - own_pair, z + 1 - 2 * (z % 2)]
 
     def plane_id(peer):
         return {"kv": peer[0] * 16 + z * 4 + peer[1]}
@@ -81,6 +81,14 @@
     l_qn.wait()
     l_qr.wait()
     l_uk.wait()
+    low_half = lax.broadcasted_iota(jnp.int32, (8, 1), 0) < 4
+
+    def halves(left, right):
+        return (
+            jnp.where(low_half, left, pltpu.roll(right, 4, 0)),
+            jnp.where(low_half, pltpu.roll(left, 4, 0), right),
+        )
+
     qx[...] = jnp.zeros((8, 128), F32)
     for step in range(STEPS):
         qx[step * 2 : step * 2 + 2, :] = qn_v[step, 0].astype(F32)
@@ -91,22 +99,25 @@
         jnp.dot(lhs, uk_v[0], preferred_element_type=F32),
         jnp.dot(lhs, uk_v[1], preferred_element_type=F32),
     )
-    zq[z, 0:4, 0:LAT] = lat[0:4].astype(BF16).astype(F32)
+    quarters = [lat[:, k * 128 : k * 128 + 128] for k in range(4)]
+    qs[me, 0:16, :] = jnp.concatenate(
+        [halves(*quarters[:2])[0], halves(*quarters[2:])[0]], axis=0
+    ).astype(BF16)
     lane = lax.broadcasted_iota(jnp.int32, (2, ROPE), 1)
     for step in range(STEPS):
         flag = jnp.where(lane == step, 1.0, 0.0).astype(F32)
-        zq[z, step * 2 : step * 2 + 2, LAT:] = jnp.concatenate(
-            [qr_v[step, 0].astype(F32), flag], axis=1
-        )
+        qx[step * 2 : step * 2 + 2, :] = jnp.concatenate([qr_v[step, 0].astype(F32), flag], axis=1)
+    tail = qx[...]
+    qs[me, 16:32, :] = jnp.concatenate([tail, tail], axis=0).astype(BF16)
 
     pl.semaphore_wait(barrier, len(in_plane) + len(in_line))
 
-    def remote(src, dst, phase, device):
+    def remote(src, dst, sent, arrived, device):
         copy = pltpu.make_async_remote_copy(
             src_ref=src,
             dst_ref=dst,
-            send_sem=send_sem.at[phase],
-            recv_sem=recv_sem.at[phase],
+            send_sem=send_sem.at[sent],
+            recv_sem=recv_sem.at[arrived],
             device_id=device,
             device_id_type=MESH,
         )
@@ -115,9 +126,13 @@
     def take(ref, sem):
         pltpu.make_async_copy(ref, ref, sem).wait()
 
-    mine = zq.at[z, pl.ds(0, 4)]
+    def slab(owner_z):
+        return qs.at[y * 16 + owner_z * 4 + x, pl.ds(0, ASKED)]
+
     for peer in in_line:
-        remote(mine, mine, 0, line_id(peer))
+        remote(slab(z), slab(z), 0, z, line_id(peer))
+    for peer in in_plane:
+        remote(slab(z), slab(z), 1, 4, plane_id(peer))
 
     l_ctx.wait()
     l_new.wait()
@@ -139,24 +154,40 @@
         keys[WIDE:, here] = mask.astype(BF16)
         return 0
 
-    lax.fori_loop(0, 4, prepare, 0)
-
-    take(zq.at[pl.ds(0, 3), pl.ds(0, 4)], recv_sem.at[0])
-    mine = q_all.at[pl.ds(pl.multiple_of(plane * 16, 16), 16)]
-    mine[...] = jnp.concatenate([zq[k, 0:4, :] for k in range(4)], axis=0).astype(BF16)
-    for peer in in_plane:
-        remote(mine, mine, 1, plane_id(peer))
-    lax.fori_loop(4, 8, prepare, 0)
+    def unpack(z_pair):
+        for to_y in range(4):
+            for to_x in range(4):
+                owner = to_y * 16 + z_pair * 8 + to_x
+                parts = [[qs[owner + j, k * 8 : k * 8 + 8, :].astype(F32) for k in range(3)] for j in (0, 4)]
+                eight = pl.ds(pl.multiple_of((to_y * 4 + to_x) * 16 + z_pair * 8, 8), 8)
+                for k in range(3):
+                    pieces = halves(parts[0][k], parts[1][k])
+                    q_all[eight, k * 256 : k * 256 + 128] = pieces[0]
+                    if k < 2:
+                        q_all[eight, k * 256 + 128 : k * 256 + 256] = pieces[1]
+
+    done = 0
+    for k, chunks in ((2, 2), (1, 1), (0, 1)):
+        lax.fori_loop(done, done + chunks, prepare, 0)
+        done += chunks
+        take(slab(in_line[k]), recv_sem.at[in_line[k]])
+        for peer in in_plane:
+            remote(slab(in_line[k]), slab(in_line[k]), 1, 7 - k, plane_id(peer))
+    lax.fori_loop(done, 8, prepare, 0)
     column = lax.broadcasted_iota(jnp.int32, (128, 1024), 1) // 16
     place = lax.broadcasted_iota(jnp.int32, (128, 1024), 0)
     spread[...] = jnp.where(column == place, 1.0, 0.0).astype(BF16)
-    take(q_all.at[pl.ds(0, 240)], recv_sem.at[1])
+    for k in range(4):
+        take(qs.at[pl.ds(0, 15), pl.ds(0, ASKED)], recv_sem.at[4 + k])
+        if k == 1:
+            unpack(own_pair)
+    unpack(1 - own_pair)
 
     scale = math.log2(math.e) * (128 + ROPE) ** -0.5
 
     def attend(part):
         blocks = [pl.ds(pl.multiple_of(to_y * 64, 64), 64) for to_y in part]
-        queries = jnp.concatenate([q_all[block, :] for block in blocks], axis=0)
+        queries = jnp.concatenate([q_all[block, :] for block in blocks], axis=0).astype(BF16)
         peak = None
         for k in range(4):
             tiles = jnp.dot(queries, keys[:, k * 512 : k * 512 + 512], preferred_element_type=F32)
@@ -180,16 +211,6 @@
             vals[block, :] = value[k * 64 : k * 64 + 64]
             stats[block, :] = note[k * 64 : k * 64 + 64]
 
-    low_half = lax.broadcasted_iota(jnp.int32, (8, 1), 0) < 4
-
-    def halves(left, right):
-        return (
-            jnp.where(low_half, left, pltpu.roll(right, 4, 0)),
-            jnp.where(low_half, pltpu.roll(left, 4, 0), right),
-        )
-
-    own_pair = z // 2
-
     def deliver(part, z_pair, last=False):
         for dy, to_y in enumerate(part):
             for dx in (2, 1, 3, 0):
@@ -210,7 +231,7 @@
                     if last and dy == 1 and dx == 0 and j == 0:
                         rb[me] = ob[me]
                     else:
-                        remote(ob.at[peer, pl.ds(0, SENT)], rb.at[me, pl.ds(0, SENT)], 2, {"kv": peer})
+                        remote(ob.at[peer, pl.ds(0, SENT)], rb.at[me, pl.ds(0, SENT)], 2, 8, {"kv": peer})
 
     far = ((y + 2) % 4, (y + 3) % 4)
     near = ((y + 1) % 4, y)
@@ -222,7 +243,7 @@
     deliver(near, own_pair, last=True)
     l_uv.wait()
     l_w.wait()
-    take(rb.at[pl.ds(0, 63), pl.ds(0, SENT)], recv_sem.at[2])
+    take(rb.at[pl.ds(0, 63), pl.ds(0, SENT)], recv_sem.at[8])
     notes = jnp.concatenate(
         [rb[k, 16:18, :].astype(F32)[0:1] for k in range(64)] + [jnp.zeros((64, 128), F32)], axis=0
     ).T
@@ -267,13 +288,13 @@
                     if z_pair is own_pair and dy == 0 and dx == 0 and dz == 0:
                         tr[me, 0:2, :] = ts[me, 0:2, :]
                     else:
-                        remote(ts.at[peer, pl.ds(0, 2)], tr.at[me, pl.ds(0, 2)], 3, {"kv": peer})
-    take(tr.at[pl.ds(0, 63), pl.ds(0, 2)], recv_sem.at[3])
+                        remote(ts.at[peer, pl.ds(0, 2)], tr.at[me, pl.ds(0, 2)], 3, 9, {"kv": peer})
+    take(tr.at[pl.ds(0, 63), pl.ds(0, 2)], recv_sem.at[9])
     result = jnp.sum(tr[:, 0:2, :], axis=0)
     out[0] = result[:, 0:112].astype(BF16)
 
-    take(zq.at[pl.ds(0, 3), pl.ds(0, 4)], send_sem.at[0])
-    take(q_all.at[pl.ds(0, 240)], send_sem.at[1])
+    take(qs.at[pl.ds(0, 3), pl.ds(0, ASKED)], send_sem.at[0])
+    take(qs.at[pl.ds(0, 60), pl.ds(0, ASKED)], send_sem.at[1])
     take(ob.at[pl.ds(0, 63), pl.ds(0, SENT)], send_sem.at[2])
     take(ts.at[pl.ds(0, 63), pl.ds(0, 2)], send_sem.at[3])
 
@@ -294,8 +315,8 @@
             pltpu.VMEM((1, 2, WIDE), BF16),
             pltpu.VMEM((1, 1), jnp.int32),
             pltpu.VMEM((8, 128), F32),
-            pltpu.VMEM((4, 8, WIDE_PAD), F32),
-            pltpu.VMEM((256, WIDE_PAD), BF16),
+            pltpu.VMEM((64, 32, 128), BF16),
+            pltpu.VMEM((256, WIDE_PAD), F32),
             pltpu.VMEM((WIDE_PAD, 2048), BF16),
             pltpu.VMEM((2048, LAT), BF16),
             pltpu.VMEM((128, 2048), F32),
@@ -308,7 +329,7 @@
             pltpu.VMEM((64, 8, 128), F32),
             pltpu.SemaphoreType.DMA((8,)),
             pltpu.SemaphoreType.DMA((4,)),
-            pltpu.SemaphoreType.DMA((4,)),
+            pltpu.SemaphoreType.DMA((10,)),
         ],
         compiler_params=pltpu.CompilerParams(
             collective_id=0, has_side_effects=True, vmem_limit_bytes=60 << 20

time: 34.2 us -> 33.4 us (0.977)
  Pallas kernels: 32.7 us -> 31.8 us
    pallas_call x1, Pallas kernels: 32.7 us -> 31.8 us  [body(): pl.pallas_call(kernel, out_shape=pltpu.VMEM((1, STEPS, 112), BF16), in_sp...]
where the time goes in v5:
time: 33.4 us; the launch traced here: 32.9 us
  Pallas kernels  31.8 us (95%)
  between operations  0.66 us (2%)
  local copies, waits for them, and re-layouts  0.51 us (2%)
    pallas_call x1, Pallas kernels, body(): pl.pallas_call(kernel, out_shape=pltpu.VMEM((1, STEPS, 112), BF16), in_sp...  31.8 us

profile of v5, /device:TPU:2, one launch (start us, length us, event | category | flops | bytes accessed | tf_op | source)
XLA Modules:
  0.0 32.9 jit_solution(9360357719155892851)
XLA Ops:
  0.7 31.8 %shard_map.82 = bf16[1,2,112]{2,1,0:T(2,128)(2,1)S(1)} custom-call(bf16[2,1,2,128]{3,2,1,0:T(2,128)(2,1)} %q_nope.1, bf16[2,1,2,64]{3,2,1,0:T(2,128)(2,1)} %q_rope.1, bf16[2,128,512]{2,1,0:T(8,128)(2,1)} %uk.1, bf16[2,512,128]{2,1,0:T(8,128)(2,1)} %uv.1, bf16[256,7168]{1,0:T(8,128)(2,1)} %out_w.1, bf16[1,576,2048]{2,1,0:T(8,128)(2,1)} %bitcast.6, ...), custom_call_target="tpu_custom_call" | custom-call | tf_op jit(solution)/shard_map/pallas_call | solution.py:304
  32.4 0.5 %copy.10 = bf16[2,1,112]{2,0,1:T(2,128)(2,1)} copy(bf16[2,1,112]{2,0,1:T(2,128)(2,1)S(1)} %bitcast.5) | data formatting | bytes 896

commit v6 on v5

--- a/solution.py
+++ b/solution.py
@@ -44,7 +44,7 @@
 
 def kernel(
     q_nope, q_rope, uk, uv, out_w, cache, new_rows, context, out,
-    qn_v, qr_v, uk_v, uv_v, w_v, new_v, ctx_v, qx, qs, q_all, keys, latents, scores, vals, stats, ob, rb, spread, ts, tr,
+    qn_v, qr_v, uk_v, uv_v, w_v, w_p, new_v, ctx_v, qx, qs, q_all, keys, latents, scores, vals, stats, ob, rb, spread, ts, tr,
     load_sem, send_sem, recv_sem,
 ):
     me = lax.axis_index("kv")
@@ -159,7 +159,7 @@
             for to_x in range(4):
                 owner = to_y * 16 + z_pair * 8 + to_x
                 parts = [[qs[owner + j, k * 8 : k * 8 + 8, :].astype(F32) for k in range(3)] for j in (0, 4)]
-                eight = pl.ds(pl.multiple_of((to_y * 4 + to_x) * 16 + z_pair * 8, 8), 8)
+                eight = pl.ds(pl.multiple_of(z_pair * 128 + (to_y * 4 + to_x) * 8, 8), 8)
                 for k in range(3):
                     pieces = halves(parts[0][k], parts[1][k])
                     q_all[eight, k * 256 : k * 256 + 128] = pieces[0]
@@ -177,17 +177,12 @@
     column = lax.broadcasted_iota(jnp.int32, (128, 1024), 1) // 16
     place = lax.broadcasted_iota(jnp.int32, (128, 1024), 0)
     spread[...] = jnp.where(column == place, 1.0, 0.0).astype(BF16)
-    for k in range(4):
-        take(qs.at[pl.ds(0, 15), pl.ds(0, ASKED)], recv_sem.at[4 + k])
-        if k == 1:
-            unpack(own_pair)
-    unpack(1 - own_pair)
 
     scale = math.log2(math.e) * (128 + ROPE) ** -0.5
 
-    def attend(part):
-        blocks = [pl.ds(pl.multiple_of(to_y * 64, 64), 64) for to_y in part]
-        queries = jnp.concatenate([q_all[block, :] for block in blocks], axis=0).astype(BF16)
+    def attend(z_pair):
+        half = pl.ds(pl.multiple_of(z_pair * 128, 128), 128)
+        queries = q_all[half, :].astype(BF16)
         peak = None
         for k in range(4):
             tiles = jnp.dot(queries, keys[:, k * 512 : k * 512 + 512], preferred_element_type=F32)
@@ -206,43 +201,55 @@
             value = value + jnp.dot(
                 expo.astype(BF16), latents[k * 512 : k * 512 + 512, :], preferred_element_type=F32
             )
-        note = with_stats(peak, jnp.sum(total, axis=1, keepdims=True), 128)
-        for k, block in enumerate(blocks):
-            vals[block, :] = value[k * 64 : k * 64 + 64]
-            stats[block, :] = note[k * 64 : k * 64 + 64]
-
-    def deliver(part, z_pair, last=False):
-        for dy, to_y in enumerate(part):
-            for dx in (2, 1, 3, 0):
-                to_x = (x + dx) % 4
-                eight = pl.ds(pl.multiple_of(((to_y * 4 + to_x) * 2 + z_pair) * 8, 8), 8)
-                quarters = [vals[eight, k * 128 : k * 128 + 128] for k in range(4)]
-                first, second = zip(halves(*quarters[:2]), halves(*quarters[2:]))
-                note = stats[eight, :]
-                note = note + pltpu.roll(note, 1, 0)
-                note = note + pltpu.roll(note, 2, 0)
-                for j, (rows, shift) in enumerate(((first, 5), (second, 1))):
-                    peer = to_y * 16 + (z_pair * 2 + j) * 4 + to_x
-                    ob[peer, 0:16, :] = jnp.concatenate(rows, axis=0).astype(BF16)
-                    moved = pltpu.roll(note, shift, 0)
-                    ob[peer, 16:32, :] = jnp.concatenate([moved, moved], axis=0).astype(BF16)
-                for j in (1, 0):
-                    peer = to_y * 16 + (z_pair * 2 + (z + j) % 2) * 4 + to_x
-                    if last and dy == 1 and dx == 0 and j == 0:
-                        rb[me] = ob[me]
-                    else:
-                        remote(ob.at[peer, pl.ds(0, SENT)], rb.at[me, pl.ds(0, SENT)], 2, 8, {"kv": peer})
-
-    far = ((y + 2) % 4, (y + 3) % 4)
-    near = ((y + 1) % 4, y)
-    attend(far)
-    deliver(far, 1 - own_pair)
-    attend(near)
-    deliver(near, 1 - own_pair)
-    deliver(far, own_pair)
-    deliver(near, own_pair, last=True)
+        vals[half, :] = value
+        stats[half, :] = with_stats(peak, jnp.sum(total, axis=1, keepdims=True), 128)
+
+    def deliver(z_pair):
+        for dy, dx in (*RING, (0, 0)):
+            to_y, to_x = (y + dy) % 4, (x + dx) % 4
+            eight = pl.ds(pl.multiple_of(z_pair * 128 + (to_y * 4 + to_x) * 8, 8), 8)
+            quarters = [vals[eight, k * 128 : k * 128 + 128] for k in range(4)]
+            first, second = zip(halves(*quarters[:2]), halves(*quarters[2:]))
+            note = stats[eight, :]
+            note = note + pltpu.roll(note, 1, 0)
+            note = note + pltpu.roll(note, 2, 0)
+            for j, (rows, shift) in enumerate(((first, 5), (second, 1))):
+                peer = to_y * 16 + (z_pair * 2 + j) * 4 + to_x
+                ob[peer, 0:16, :] = jnp.concatenate(rows, axis=0).astype(BF16)
+                moved = pltpu.roll(note, shift, 0)
+                ob[peer, 16:32, :] = jnp.concatenate([moved, moved], axis=0).astype(BF16)
+            for j in (1, 0):
+                peer = to_y * 16 + (z_pair * 2 + (z + j) % 2) * 4 + to_x
+                if z_pair is own_pair and dy == 0 and dx == 0 and j == 0:
+                    rb[me] = ob[me]
+                else:
+                    remote(ob.at[peer, pl.ds(0, SENT)], rb.at[me, pl.ds(0, SENT)], 2, 8, {"kv": peer})
+
+    def arrived(k):
+        take(qs.at[pl.ds(0, 15), pl.ds(0, ASKED)], recv_sem.at[4 + k])
+
+    arrived(0)
+    arrived(1)
+    unpack(own_pair)
+    attend(own_pair)
+    arrived(2)
+    arrived(3)
+    unpack(1 - own_pair)
+    attend(1 - own_pair)
+    deliver(1 - own_pair)
+    deliver(own_pair)
     l_uv.wait()
     l_w.wait()
+
+    def align(group, _):
+        columns = w_v[:, pl.ds(pl.multiple_of(group * 896, 128), 896)]
+        gap = jnp.zeros((256, 16), BF16)
+        w_p[:, pl.ds(pl.multiple_of(group * 1024, 128), 1024)] = jnp.concatenate(
+            [piece for j in range(8) for piece in (columns[:, j * 112 : j * 112 + 112], gap)], axis=1
+        )
+        return 0
+
+    lax.fori_loop(0, 8, align, 0)
     take(rb.at[pl.ds(0, 63), pl.ds(0, SENT)], recv_sem.at[8])
     notes = jnp.concatenate(
         [rb[k, 16:18, :].astype(F32)[0:1] for k in range(64)] + [jnp.zeros((64, 128), F32)], axis=0
@@ -275,20 +282,33 @@
     pairs = head_value + pltpu.roll(head_value, 7, 0)
     first = lax.broadcasted_iota(jnp.int32, (8, 1), 0) == 0
     flat = jnp.where(first, pairs, pltpu.roll(pairs, 7, 0)).astype(BF16)
-    for z_pair in (1 - own_pair, own_pair):
-        for dy in (2, 1, 3, 0):
-            group = ((y + dy) % 4) * 2 + z_pair
-            columns = pl.ds(pl.multiple_of(group * 896, 128), 896)
-            term = jnp.dot(flat, w_v[:, columns], preferred_element_type=F32)
-            for j in range(8):
-                ts[group * 8 + j, :, 0:112] = term[:, j * 112 : j * 112 + 112]
-            for dx in (2, 1, 3, 0):
-                for dz in (1, 0):
-                    peer = group * 8 + ((z + dz) % 2) * 4 + (x + dx) % 4
-                    if z_pair is own_pair and dy == 0 and dx == 0 and dz == 0:
-                        tr[me, 0:2, :] = ts[me, 0:2, :]
-                    else:
-                        remote(ts.at[peer, pl.ds(0, 2)], tr.at[me, pl.ds(0, 2)], 3, 9, {"kv": peer})
+    def share(z_pair, dy):
+        group = ((y + dy) % 4) * 2 + z_pair
+        columns = pl.ds(pl.multiple_of(group * 1024, 128), 1024)
+        return group, jnp.dot(flat, w_p[:, columns], preferred_element_type=F32)
+
+    def hand_out(z_pair, dy, group):
+        for dx in (2, 1, 3, 0):
+            for dz in (1, 0):
+                peer = group * 8 + ((z + dz) % 2) * 4 + (x + dx) % 4
+                if z_pair is own_pair and dy == 0 and dx == 0 and dz == 0:
+                    tr[me, 0:2, :] = ts[me, 0:2, :]
+                else:
+                    remote(ts.at[peer, pl.ds(0, 2)], tr.at[me, pl.ds(0, 2)], 3, 9, {"kv": peer})
+
+    def keep(group, term):
+        for j in range(8):
+            ts[group * 8 + j] = term[:, j * 128 : j * 128 + 128]
+
+    order = [(z_pair, dy) for z_pair in (1 - own_pair, own_pair) for dy in (2, 1, 3, 0)]
+    group, term = share(*order[0])
+    keep(group, term)
+    for k in range(8):
+        later = share(*order[k + 1]) if k < 7 else None
+        hand_out(*order[k], group)
+        if later:
+            group, term = later
+            keep(group, term)
     take(tr.at[pl.ds(0, 63), pl.ds(0, 2)], recv_sem.at[9])
     result = jnp.sum(tr[:, 0:2, :], axis=0)
     out[0] = result[:, 0:112].astype(BF16)
@@ -312,6 +332,7 @@
             pltpu.VMEM((2, 128, LAT), BF16),
             pltpu.VMEM((2, LAT, 128), BF16),
             pltpu.VMEM((256, 7168), BF16),
+            pltpu.VMEM((256, 8192), BF16),
             pltpu.VMEM((1, 2, WIDE), BF16),
             pltpu.VMEM((1, 1), jnp.int32),
             pltpu.VMEM((8, 128), F32),

time: 33.4 us -> 33 us (0.988); the launches traced: 32.9 us -> 32.9 us
  no operation moved by 1% of the time
where the time goes in v6:
time: 33 us; the launch traced here: 32.9 us
  Pallas kernels  31.7 us (96%)
  between operations  0.66 us (2%)
  local copies, waits for them, and re-layouts  0.51 us (2%)
    pallas_call x1, Pallas kernels, body(): pl.pallas_call(kernel, out_shape=pltpu.VMEM((1, STEPS, 112), BF16), in_sp...  31.7 us

profile of v6, /device:TPU:2, one launch (start us, length us, event | category | flops | bytes accessed | tf_op | source)
XLA Modules:
  0.0 32.9 jit_solution(10014762135023693711)
XLA Ops:
  0.7 31.7 %shard_map.82 = bf16[1,2,112]{2,1,0:T(2,128)(2,1)S(1)} custom-call(bf16[2,1,2,128]{3,2,1,0:T(2,128)(2,1)} %q_nope.1, bf16[2,1,2,64]{3,2,1,0:T(2,128)(2,1)} %q_rope.1, bf16[2,128,512]{2,1,0:T(8,128)(2,1)} %uk.1, bf16[2,512,128]{2,1,0:T(8,128)(2,1)} %uv.1, bf16[256,7168]{1,0:T(8,128)(2,1)} %out_w.1, bf16[1,576,2048]{2,1,0:T(8,128)(2,1)} %bitcast.6, ...), custom_call_target="tpu_custom_call" | custom-call | tf_op jit(solution)/shard_map/pallas_call | solution.py:324
  32.4 0.5 %copy.10 = bf16[2,1,112]{2,0,1:T(2,128)(2,1)} copy(bf16[2,1,112]{2,0,1:T(2,128)(2,1)S(1)} %bitcast.5) | data formatting | bytes 896

commit v7 on v6

--- a/solution.py
+++ b/solution.py
@@ -62,7 +62,7 @@
     loads = [
         pltpu.make_async_copy(src, dst, load_sem.at[k])
         for k, (src, dst) in enumerate(
-            [(q_nope, qn_v), (q_rope, qr_v), (uk, uk_v), (context, ctx_v), (new_rows, new_v), (cache.at[0], keys.at[pl.ds(0, WIDE)]), (uv, uv_v), (out_w, w_v)]
+            [(q_nope, qn_v), (q_rope, qr_v), (uk, uk_v), (context, ctx_v), (new_rows, new_v), (cache.at[0], keys.at[pl.ds(0, WIDE)]), (uv.at[0], uv_v.at[:, pl.ds(0, 128)]), (out_w, w_v), (uv.at[1], uv_v.at[:, pl.ds(128, 128)])]
         )
     ]
     barrier = pltpu.get_barrier_semaphore()
@@ -76,7 +76,7 @@
         load.start()
     for load in loads[3:]:
         load.start()
-    l_qn, l_qr, l_uk, l_ctx, l_new, l_cache, l_uv, l_w = loads
+    l_qn, l_qr, l_uk, l_ctx, l_new, l_cache, l_uv, l_w, l_uv2 = loads
 
     l_qn.wait()
     l_qr.wait()
@@ -202,7 +202,9 @@
                 expo.astype(BF16), latents[k * 512 : k * 512 + 512, :], preferred_element_type=F32
             )
         vals[half, :] = value
-        stats[half, :] = with_stats(peak, jnp.sum(total, axis=1, keepdims=True), 128)
+        note = with_stats(peak, jnp.sum(total, axis=1, keepdims=True), 128)
+        note = note + pltpu.roll(note, 1, 0)
+        stats[half, :] = note + pltpu.roll(note, 2, 0)
 
     def deliver(z_pair):
         for dy, dx in (*RING, (0, 0)):
@@ -211,8 +213,6 @@
             quarters = [vals[eight, k * 128 : k * 128 + 128] for k in range(4)]
             first, second = zip(halves(*quarters[:2]), halves(*quarters[2:]))
             note = stats[eight, :]
-            note = note + pltpu.roll(note, 1, 0)
-            note = note + pltpu.roll(note, 2, 0)
             for j, (rows, shift) in enumerate(((first, 5), (second, 1))):
                 peer = to_y * 16 + (z_pair * 2 + j) * 4 + to_x
                 ob[peer, 0:16, :] = jnp.concatenate(rows, axis=0).astype(BF16)
@@ -239,6 +239,7 @@
     deliver(1 - own_pair)
     deliver(own_pair)
     l_uv.wait()
+    l_uv2.wait()
     l_w.wait()
 
     def align(group, _):
@@ -272,13 +273,8 @@
         [top, pltpu.roll(top, 4, 0), bottom, pltpu.roll(bottom, 4, 0)], axis=1
     ).astype(BF16)
 
-    head_value = jnp.concatenate(
-        [
-            jnp.where(even, jnp.dot(latent, uv_v[0], preferred_element_type=F32), 0.0),
-            jnp.where(even, 0.0, jnp.dot(latent, uv_v[1], preferred_element_type=F32)),
-        ],
-        axis=1,
-    )
+    own_head = (lax.broadcasted_iota(jnp.int32, (8, 256), 1) < 128) == even
+    head_value = jnp.where(own_head, jnp.dot(latent, uv_v[...], preferred_element_type=F32), 0.0)
     pairs = head_value + pltpu.roll(head_value, 7, 0)
     first = lax.broadcasted_iota(jnp.int32, (8, 1), 0) == 0
     flat = jnp.where(first, pairs, pltpu.roll(pairs, 7, 0)).astype(BF16)
@@ -330,7 +326,7 @@
             pltpu.VMEM((2, 1, 2, 128), BF16),
             pltpu.VMEM((2, 1, 2, ROPE), BF16),
             pltpu.VMEM((2, 128, LAT), BF16),
-            pltpu.VMEM((2, LAT, 128), BF16),
+            pltpu.VMEM((LAT, 256), BF16),
             pltpu.VMEM((256, 7168), BF16),
             pltpu.VMEM((256, 8192), BF16),
             pltpu.VMEM((1, 2, WIDE), BF16),
@@ -348,7 +344,7 @@
             pltpu.VMEM((128, 1024), BF16),
             pltpu.VMEM((64, 8, 128), F32),
             pltpu.VMEM((64, 8, 128), F32),
-            pltpu.SemaphoreType.DMA((8,)),
+            pltpu.SemaphoreType.DMA((9,)),
             pltpu.SemaphoreType.DMA((4,)),
             pltpu.SemaphoreType.DMA((10,)),
         ],

time: 33 us -> 33 us (level)
  no operation moved by 1% of the time
where the time goes in v7:
time: 33 us; the launch traced here: 32.9 us
  Pallas kernels  31.8 us (96%)
  between operations  0.66 us (2%)
  local copies, waits for them, and re-layouts  0.51 us (2%)
    pallas_call x1, Pallas kernels, body(): pl.pallas_call(kernel, out_shape=pltpu.VMEM((1, STEPS, 112), BF16), in_sp...  31.8 us

profile of v7, /device:TPU:2, one launch (start us, length us, event | category | flops | bytes accessed | tf_op | source)
XLA Modules:
  0.0 32.9 jit_solution(18423960290705391452)
XLA Ops:
  0.7 31.8 %shard_map.82 = bf16[1,2,112]{2,1,0:T(2,128)(2,1)S(1)} custom-call(bf16[2,1,2,128]{3,2,1,0:T(2,128)(2,1)} %q_nope.1, bf16[2,1,2,64]{3,2,1,0:T(2,128)(2,1)} %q_rope.1, bf16[2,128,512]{2,1,0:T(8,128)(2,1)} %uk.1, bf16[2,512,128]{2,1,0:T(8,128)(2,1)} %uv.1, bf16[256,7168]{1,0:T(8,128)(2,1)} %out_w.1, bf16[1,576,2048]{2,1,0:T(8,128)(2,1)} %bitcast.6, ...), custom_call_target="tpu_custom_call" | custom-call | tf_op jit(solution)/shard_map/pallas_call | solution.py:320
  32.4 0.5 %copy.10 = bf16[2,1,112]{2,0,1:T(2,128)(2,1)} copy(bf16[2,1,112]{2,0,1:T(2,128)(2,1)S(1)} %bitcast.5) | data formatting | bytes 896

commit v8 on v6

--- a/solution.py
+++ b/solution.py
@@ -184,10 +184,10 @@
         half = pl.ds(pl.multiple_of(z_pair * 128, 128), 128)
         queries = q_all[half, :].astype(BF16)
         peak = None
-        for k in range(4):
-            tiles = jnp.dot(queries, keys[:, k * 512 : k * 512 + 512], preferred_element_type=F32)
-            scores[:, k * 512 : k * 512 + 512] = tiles
-            for j in range(4):
+        for k in range(2):
+            tiles = jnp.dot(queries, keys[:, k * 1024 : k * 1024 + 1024], preferred_element_type=F32)
+            scores[:, k * 1024 : k * 1024 + 1024] = tiles
+            for j in range(8):
                 tile = tiles[:, j * 128 : j * 128 + 128]
                 peak = tile if peak is None else jnp.maximum(peak, tile)
         high, low = split(jnp.max(peak, axis=1, keepdims=True) * scale)

time: 33 us -> 33 us (level)
  no operation moved by 1% of the time
where the time goes in v8:
time: 33 us; the launch traced here: 32.9 us
  Pallas kernels  31.7 us (96%)
  between operations  0.66 us (2%)
  local copies, waits for them, and re-layouts  0.51 us (2%)
    pallas_call x1, Pallas kernels, body(): pl.pallas_call(kernel, out_shape=pltpu.VMEM((1, STEPS, 112), BF16), in_sp...  31.7 us

profile of v8, /device:TPU:2, one launch (start us, length us, event | category | flops | bytes accessed | tf_op | source)
XLA Modules:
  0.0 32.9 jit_solution(10014762135023693711)
XLA Ops:
  0.7 31.7 %shard_map.82 = bf16[1,2,112]{2,1,0:T(2,128)(2,1)S(1)} custom-call(bf16[2,1,2,128]{3,2,1,0:T(2,128)(2,1)} %q_nope.1, bf16[2,1,2,64]{3,2,1,0:T(2,128)(2,1)} %q_rope.1, bf16[2,128,512]{2,1,0:T(8,128)(2,1)} %uk.1, bf16[2,512,128]{2,1,0:T(8,128)(2,1)} %uv.1, bf16[256,7168]{1,0:T(8,128)(2,1)} %out_w.1, bf16[1,576,2048]{2,1,0:T(8,128)(2,1)} %bitcast.6, ...), custom_call_target="tpu_custom_call" | custom-call | tf_op jit(solution)/shard_map/pallas_call | solution.py:324
  32.4 0.5 %copy.10 = bf16[2,1,112]{2,0,1:T(2,128)(2,1)} copy(bf16[2,1,112]{2,0,1:T(2,128)(2,1)S(1)} %bitcast.5) | data formatting | bytes 896
